TPU v7x, 128 devices: a whole 4x4x4 slice. The times are simulated.
128 devices in a mesh: gx: 8 (over z_lo, y), gy: 16 (over x, z_hi, core).
Axes of the slice: x: 4, y: 4, z: 4 (z_hi: 2, z_lo: 2; z = z_hi * 2 + z_lo), core: 2. Of those that a mesh axis runs over, the one named last changes fastest.
Arguments:
- volume: float32 [4, 64, 128, 128], P(None, 'gx', 'gy'), may hold values from -6 to 6
- kernel_one: float32 [16, 4, 3, 3, 3], replicated, may hold values from -0.625 to 0.625
- bias_one: float32 [16], replicated, may hold values from -3 to 3
- kernel_two: float32 [32, 16, 3, 3, 3], replicated, may hold values from -0.3125 to 0.3125
- bias_two: float32 [32], replicated, may hold values from -3 to 3
- cotangent: float32 [32, 16, 1024], P('gy', 'gx'), may hold values from -6 to 6
Outputs:
- pooled: float32 [32, 16, 1024], P('gy', 'gx')
- grad_kernel_one: float32 [16, 4, 3, 3, 3], replicated
- grad_bias_one: float32 [16], replicated
- grad_kernel_two: float32 [32, 16, 3, 3, 3], replicated
- grad_bias_two: float32 [32], replicated
All inputs are finite; a program needn't handle non-finite values.
Results may differ from a plain program's by a relative error of at most 0.0003.
Values sent between devices are 32-bit elements; how exact they have to be, the bound alone decides.
No kernel may reach another device: no remote copies, remote signals or barrier semaphores. Data moves between devices by JAX's collectives and lax.ppermute only.
A program may use at most 128 MiB of HBM per device.

v0:
```python
import jax
import jax.numpy as jnp
from jax import lax
from jax.sharding import PartitionSpec as P

LAYOUT = ("NCDHW", "OIDHW", "NCDHW")


def padded(block, sides, width):
    for axis, dim in sides:
        count = lax.axis_size(axis)
        forward = [(i, i + 1) for i in range(count - 1)]
        backward = [(target, source) for source, target in forward]
        low = lax.ppermute(
            lax.slice_in_dim(block, block.shape[dim] - width, None, axis=dim), axis, forward
        )
        high = lax.ppermute(lax.slice_in_dim(block, 0, width, axis=dim), axis, backward)
        block = jnp.concatenate([low, block, high], axis=dim)
    return block


def convolve(field, kernel, padding):
    result = lax.conv_general_dilated(
        field[None],
        kernel,
        (1, 1, 1),
        padding,
        dimension_numbers=LAYOUT,
        precision=lax.Precision.HIGHEST,
    )
    return result[0]


def kernel_grad(extended, gradient):
    result = lax.conv_general_dilated(
        extended[:, None],
        gradient[:, None],
        (1, 1, 1),
        ((0, 0), (0, 0), (1, 1)),
        dimension_numbers=LAYOUT,
        precision=lax.Precision.HIGHEST,
    )
    return jnp.transpose(result, (1, 0, 2, 3, 4))


def average_cells(field):
    chans, ext_a, ext_b, ext_c = field.shape
    return field.reshape(chans, ext_a // 2, 2, ext_b // 2, 2, ext_c // 2, 2).mean(axis=(2, 4, 6))


def spread_cells(gradient):
    chans, ext_a, ext_b, ext_c = gradient.shape
    wide = jnp.broadcast_to(
        gradient[:, :, None, :, None, :, None], (chans, ext_a, 2, ext_b, 2, ext_c, 2)
    )
    return wide.reshape(chans, 2 * ext_a, 2 * ext_b, 2 * ext_c) * 0.125


def silu_slope(act):
    sigmoid_vals = jax.nn.sigmoid(act)
    return sigmoid_vals * (1.0 + act * (1.0 - sigmoid_vals))


def with_bias(field, bias):
    return field + bias[:, None, None, None]


def flipped(kernel):
    return jnp.transpose(jnp.flip(kernel, (2, 3, 4)), (1, 0, 2, 3, 4))


def extend(field):
    return padded(field, (("gx", 1), ("gy", 2)), 1)


def on_device(volume, kernel_one, bias_one, kernel_two, bias_two, cotangent):
    filters = kernel_two.shape[0]
    extent_x = volume.shape[1]
    total_x = extent_x * lax.axis_size("gx")
    depth_pad = ((0, 0), (0, 0), (1, 1))
    padded_volume = extend(volume)
    act_one = with_bias(convolve(padded_volume, kernel_one, depth_pad), bias_one)
    pooled_one = average_cells(jax.nn.silu(act_one))
    padded_pooled = extend(pooled_one)
    act_two = with_bias(convolve(padded_pooled, kernel_two, depth_pad), bias_two)
    map_two = average_cells(jax.nn.silu(act_two))
    flat_map = map_two.reshape(filters, extent_x // 4, -1)
    regrouped = lax.all_to_all(flat_map, "gy", split_axis=0, concat_axis=2, tiled=True)
    returned = lax.all_to_all(cotangent, "gy", split_axis=2, concat_axis=0, tiled=True)
    upstream = returned.reshape(map_two.shape) * (8.0 / total_x)
    grad_act_two = spread_cells(upstream) * silu_slope(act_two)
    grad_bias_two = jnp.sum(grad_act_two, axis=(1, 2, 3))
    grad_kernel_two = kernel_grad(padded_pooled, grad_act_two)
    padded_grad = extend(grad_act_two)
    grad_pooled = convolve(padded_grad, flipped(kernel_two), depth_pad)
    grad_act_one = spread_cells(grad_pooled) * silu_slope(act_one)
    grad_bias_one = jnp.sum(grad_act_one, axis=(1, 2, 3))
    grad_kernel_one = kernel_grad(padded_volume, grad_act_one)
    totals = lax.psum(
        (grad_kernel_one, grad_bias_one, grad_kernel_two, grad_bias_two), ("gx", "gy")
    )
    return (regrouped, totals[0], totals[1], totals[2], totals[3])


def solution(mesh):
    in_specs = (P(None, "gx", "gy", None), P(), P(), P(), P(), P("gy", "gx", None))
    out_specs = (P("gy", "gx", None), P(), P(), P(), P())
    return jax.shard_map(
        on_device, mesh=mesh, in_specs=in_specs, out_specs=out_specs, check_vma=False
    )
```

profile of v0, /device:TPU:0, one launch (start us, length us, event | category | flops | bytes accessed | tf_op | source)
XLA Modules:
  0.0 600.5 jit_solution(8392210926758060067)
XLA Ops:
  1.4 3.6 collective-permute-start
  7.3 3.3 collective-permute-done.1
  18.7 9.3 %pad_maximum_fusion = (f32[4,10,10,128]{0,3,2,1:T(8,128)}, f32[4,10,10,1,128]{0,4,2,1,3:T(8,128)}) fusion(f32[4,10,1,128]{0,3,2,1:T(8,128)S(1)} %copy.248, f32[4,10,8,128]{0,3,2,1:T(8,128)} %copy.247, f32[4,10,1,128]{0,3,2,1:T(8,128)S(1)} %copy.246), kind=kLoop, calls=%fused_computation | loop fusion | flops 102400 | bytes 614400 | tf_op jit(solution)/shard_map/concatenate | solution.py:18
  28.0 4.7 copy.300
  33.6 4.0 copy.251
  41.5 98.8 %fusion.3 = f32[8,8,8,17,16]{4,2,3,1,0:T(8,128)} fusion(f32[16,4,3,3,3]{0,1,4,3,2:T(4,128)S(1)} %copy-done.14, f32[4,10,10,8,19]{3,0,4,2,1:T(4,128)S(1)} %fusion.61), kind=kOutput, calls=%fused_computation.7 | convolution fusion | flops 180486144 | bytes 807168 | tf_op jit(solution)/shard_map/conv_general_dilated | solution.py:23
  140.3 6.4 %copy.252 = f32[8,8,8,17,16]{3,4,2,1,0:T(8,128)} copy(f32[8,8,8,17,16]{4,2,3,1,0:T(8,128)} %fusion.3) | data formatting | bytes 1114112 | tf_op jit(solution)/shard_map/conv_general_dilated | solution.py:23
  146.7 5.8 add_multiply_fusion
  152.5 3.9 copy.253
  156.4 3.3 reshape.164
  162.5 5.2 copy.255
  169.7 4.6 collective-permute-start.4
  176.3 16.2 %all_to_all.27 = f32[16,1,256]{2,1,0:T(1,128)S(1)} all-to-all(f32[16,1,256]{2,1,0:T(1,128)S(1)} %reshape.204), channel_id=1, replica_groups=mesh['gx'=8,'gy'=16] {'gy'}, dimensions={0} | all-to-all | bytes 32768 | tf_op jit(solution)/shard_map/all_to_all | solution.py:89
  202.8 6.8 %copy.291 = f32[8,8,8,17,16]{4,3,2,1,0:T(8,128)} copy(f32[8,8,8,17,16]{3,4,2,1,0:T(8,128)} %get-tuple-element.11) | data formatting | bytes 1114112 | tf_op jit(solution)/shard_map/mul | solution.py:61
  209.6 6.5 %reshape.201 = f32[8,8,1,136,16]{4,3,1,0,2:T(8,128)} reshape(f32[8,8,8,17,16]{4,3,2,1,0:T(8,128)} %copy.291) | data formatting | bytes 1114112 | tf_op jit(solution)/shard_map/mul | solution.py:61
  220.9 9.0 %add_multiply_fusion.1 = (f32[4,4,8,9,32]{4,2,3,1,0:T(8,128)}, f32[4,4,8,9,32]{4,2,3,1,0:T(8,128)S(1)}) fusion(f32[32]{0:T(128)S(1)} %copy-done.11, f32[32,16,3,3,3]{0,1,4,3,2:T(8,128)S(1)} %copy-done, f32[16,6,6,1,7,2]{0,4,5,2,1,3:T(8,128)S(1)} %slice.62, f32[16,6,6,1,8,9]{0,4,5,2,1,3:T(8,128)} %copy.261, pred[8,9]{0,1:T(8,128)(4,1)S(1)} %copy-done.15), kind=kOutput, calls=%fused_computation.35 | convolution fusion | flops 191586816 | bytes 548552 | tf_op jit(solution)/shard_map/conv_general_dilated | solution.py:23
  231.7 5.9 all-to-all-start
  239.1 4.5 collective-permute-start.8
  244.8 30.8 %fusion.50 = f32[32,16,3,3,3]{0,1,4,3,2:T(8,128)} fusion(f32[16,1,6,6,64]{0,1,4,3,2:T(1,128)S(1)} %bitcast.120, f32[32,1,4,4,64]{0,1,4,3,2:T(1,128)S(1)} %copy.287), kind=kOutput, calls=%fused_computation.77 | convolution fusion | flops 168099840 | bytes 333824 | tf_op jit(solution)/shard_map/transpose | solution.py:43
  284.4 13.4 %fusion.25 = f32[4,4,8,9,16]{4,2,3,1,0:T(8,128)S(1)} fusion(f32[32,16,3,3,3]{0,1,4,3,2:T(8,128)S(1)} %copy-done, f32[32,6,6,1,7,2]{0,4,5,2,1,3:T(8,128)S(1)} %slice.66, f32[32,6,6,1,8,9]{0,4,5,2,1,3:T(8,128)S(1)} %copy.278, pred[8,9]{0,1:T(8,128)(4,1)S(1)} %copy-done.15), kind=kOutput, calls=%fused_computation.28 | convolution fusion | flops 191443968 | bytes 525384 | tf_op jit(solution)/shard_map/conv_general_dilated | solution.py:23
  299.2 4.0 broadcast_in_dim.39
  306.3 6.9 %copy.282 = f32[16,1,8,8,128]{0,1,4,3,2:T(1,128)} copy(f32[16,1,8,8,128]{4,0,3,2,1:T(8,128)S(1)} %multiply_multiply_fusion) | data formatting | bytes 1048576 | tf_op jit(solution)/shard_map/mul | solution.py:96
  313.2 205.4 %fusion.49 = f32[16,4,3,3,3]{0,1,4,3,2:T(4,128)S(1)} fusion(f32[4,1,10,10,128]{0,1,4,3,2:T(1,128)} %bitcast.110, f32[16,1,8,8,128]{0,1,4,3,2:T(1,128)} %copy.282), kind=kOutput, calls=%fused_computation.76 | convolution fusion | flops 168984576 | bytes 736000 | tf_op jit(solution)/shard_map/transpose | solution.py:43
  519.8 80.5 %all-reduce = (f32[16,4,3,3,3]{0,1,4,3,2:T(4,128)}, f32[16]{0:T(128)}, f32[32,16,3,3,3]{0,1,4,3,2:T(8,128)}, f32[32]{0:T(128)}) all-reduce(f32[16,4,3,3,3]{0,1,4,3,2:T(4,128)S(1)} %fusion.49, f32[16]{0:T(128)S(1)} %fusion.1, f32[32,16,3,3,3]{0,1,4,3,2:T(8,128)S(1)} %copy-done.8, ...), channel_id=1, replica_groups=mesh['gx'=8,'gy'=16] {'gx','gy'}, use_global_device_ids=true, to_apply=%region_2.3 | all-reduce | flops 15600 | bytes 124800 | tf_op jit(solution)/shard_map/psum | solution.py:99
  (131 shorter events, 56.0 us)
Async XLA Ops:
  0.6 220.2 %copy-start = (f32[32,16,3,3,3]{0,1,4,3,2:T(8,128)S(1)}, f32[32,16,3,3,3]{0,1,4,3,2:T(8,128)}, u32[]{:S(2)}) copy-start(f32[32,16,3,3,3]{0,1,4,3,2:T(8,128)} %param.9) | copy-start | bytes 165892
  1.4 5.0 collective-permute-start
  5.0 5.6 collective-permute-start.1
  10.7 7.5 %collective-permute-start.3 = (f32[4,10,1,128]{3,0,2,1:T(4,128)S(1)}, f32[4,10,1,128]{3,0,2,1:T(4,128)S(1)}, u32[]{:S(2)}, u32[]{:S(2)}) collective-permute-start(f32[4,10,1,128]{3,0,2,1:T(4,128)S(1)} %copy.297), channel_id=1, source_target_pairs={{1,0},{2,1},{3,2},{4,3},{5,4},{6,5},{7,6},{8,7},{9,8},{10,9},{11,1... | collective-permute-start | bytes 61448 | tf_op jit(solution)/shard_map/ppermute | solution.py:17
  12.0 6.4 %collective-permute-start.2 = (f32[4,10,1,128]{3,0,2,1:T(4,128)S(1)}, f32[4,10,1,128]{3,0,2,1:T(4,128)S(1)}, u32[]{:S(2)}, u32[]{:S(2)}) collective-permute-start(f32[4,10,1,128]{3,0,2,1:T(4,128)S(1)} %copy.296), channel_id=1, source_target_pairs={{0,1},{1,2},{2,3},{3,4},{4,5},{5,6},{6,7},{7,8},{8,9},{9,10},{10,1... | collective-permute-start | bytes 61448 | tf_op jit(solution)/shard_map/ppermute | solution.py:14
  140.3 6.4 %copy-start.10 = (f32[16]{0:T(128)S(1)}, f32[16]{0:T(128)}, u32[]{:S(2)}) copy-start(f32[16]{0:T(128)} %param.8) | copy-start | bytes 196
  140.3 6.4 %copy-start.13 = (pred[8,17]{1,0:T(8,128)(4,1)S(1)}, pred[8,17]{1,0:T(8,128)(4,1)}, u32[]{:S(2)}) copy-start(pred[8,17]{1,0:T(8,128)(4,1)} %constant.36) | copy-start | bytes 412
  159.8 7.9 %copy-start.4 = (f32[8,8,1,136,16]{3,4,1,0,2:T(8,128)}, f32[8,8,1,136,16]{3,4,1,0,2:T(8,128)S(1)}, u32[]{:S(2)}) copy-start(f32[8,8,1,136,16]{3,4,1,0,2:T(8,128)S(1)} %reshape.164) | copy-start | bytes 1671172
  162.5 11.8 %copy-start.9 = (f32[2,2,1024]{2,1,0:T(2,128)S(1)}, f32[2,2,1024]{2,1,0:T(2,128)}, u32[]{:S(2)}) copy-start(f32[2,2,1024]{2,1,0:T(2,128)} %param.11) | copy-start | bytes 49156
  168.4 27.1 %collective-permute-start.5 = (f32[16,1,4,64]{0,3,2,1:T(8,128)S(1)}, f32[16,1,4,64]{0,3,2,1:T(8,128)S(1)}, u32[]{:S(2)}, u32[]{:S(2)}) collective-permute-start(f32[16,1,4,64]{0,3,2,1:T(8,128)S(1)} %get-tuple-element.14), channel_id=1, source_target_pairs={{16,0},{32,16},{48,32},{64,48},{80,64},{96,80},{112,96},{17,1},{33... | collective-permute-start | bytes 49160 | tf_op jit(solution)/shard_map/ppermute | solution.py:17
  169.7 25.9 %collective-permute-start.4 = (f32[16,1,4,64]{0,3,2,1:T(8,128)S(1)}, f32[16,1,4,64]{0,3,2,1:T(8,128)S(1)}, u32[]{:S(2)}, u32[]{:S(2)}) collective-permute-start(f32[16,1,4,64]{0,3,2,1:T(8,128)S(1)} %get-tuple-element.13), channel_id=1, source_target_pairs={{0,16},{16,32},{32,48},{48,64},{64,80},{80,96},{96,112},{1,17},{17... | collective-permute-start | bytes 49160 | tf_op jit(solution)/shard_map/ppermute | solution.py:14
  195.7 20.4 %collective-permute-start.7 = (f32[16,6,1,64]{3,0,2,1:T(8,128)S(1)}, f32[16,6,1,64]{3,0,2,1:T(8,128)S(1)}, u32[]{:S(2)}, u32[]{:S(2)}) collective-permute-start(f32[16,6,1,64]{3,0,2,1:T(8,128)S(1)} %get-tuple-element.22), channel_id=1, source_target_pairs={{1,0},{2,1},{3,2},{4,3},{5,4},{6,5},{7,6},{8,7},{9,8},{10,9},{11,1... | collective-permute-start | bytes 73736 | tf_op jit(solution)/shard_map/ppermute | solution.py:17
  197.0 19.1 %collective-permute-start.6 = (f32[16,6,1,64]{3,0,2,1:T(8,128)S(1)}, f32[16,6,1,64]{3,0,2,1:T(8,128)S(1)}, u32[]{:S(2)}, u32[]{:S(2)}) collective-permute-start(f32[16,6,1,64]{3,0,2,1:T(8,128)S(1)} %get-tuple-element.21), channel_id=1, source_target_pairs={{0,1},{1,2},{2,3},{3,4},{4,5},{5,6},{6,7},{7,8},{8,9},{9,10},{10,1... | collective-permute-start | bytes 73736 | tf_op jit(solution)/shard_map/ppermute | solution.py:14
  229.9 7.8 %copy-start.6 = (f32[32,4,4,64]{3,0,2,1:T(8,128)S(1)}, f32[32,4,4,64]{3,0,2,1:T(8,128)}, u32[]{:S(2)}) copy-start(f32[32,4,4,64]{3,0,2,1:T(8,128)} %copy.275) | copy-start | bytes 393220
  231.7 49.5 %all-to-all-start = ((f32[16,1,256]{2,1,0:T(1,128)}), f32[16,1,256]{2,1,0:T(1,128)S(1)}, u32[]{:S(2)}, u32[]{:S(2)}) async-start(f32[16,1,256]{2,1,0:T(1,128)} %reshape.202), calls=%async_computation | async-start | bytes 32768 | tf_op jit(solution)/shard_map/all_to_all | solution.py:88
  237.8 38.0 %collective-permute-start.9 = (f32[32,1,4,64]{3,0,2,1:T(8,128)S(1)}, f32[32,1,4,64]{3,0,2,1:T(8,128)S(1)}, u32[]{:S(2)}, u32[]{:S(2)}) collective-permute-start(f32[32,1,4,64]{3,0,2,1:T(8,128)S(1)} %get-tuple-element.20), channel_id=1, source_target_pairs={{16,0},{32,16},{48,32},{64,48},{80,64},{96,80},{112,96},{17,1},{33... | collective-permute-start | bytes 98312 | tf_op jit(solution)/shard_map/ppermute | solution.py:17
  239.1 36.7 %collective-permute-start.8 = (f32[32,1,4,64]{3,0,2,1:T(8,128)S(1)}, f32[32,1,4,64]{3,0,2,1:T(8,128)S(1)}, u32[]{:S(2)}, u32[]{:S(2)}) collective-permute-start(f32[32,1,4,64]{3,0,2,1:T(8,128)S(1)} %get-tuple-element.19), channel_id=1, source_target_pairs={{0,16},{16,32},{32,48},{48,64},{64,80},{80,96},{96,112},{1,17},{17... | collective-permute-start | bytes 98312 | tf_op jit(solution)/shard_map/ppermute | solution.py:14
  244.8 30.8 %copy-start.7 = (f32[4,4,8,9,32]{4,2,3,1,0:T(8,128)S(1)}, f32[4,4,8,9,32]{4,2,3,1,0:T(8,128)}, u32[]{:S(2)}) copy-start(f32[4,4,8,9,32]{4,2,3,1,0:T(8,128)} %get-tuple-element.27) | copy-start | bytes 442372
  275.8 6.8 %collective-permute-start.11 = (f32[32,6,1,64]{3,0,2,1:T(8,128)S(1)}, f32[32,6,1,64]{3,0,2,1:T(8,128)S(1)}, u32[]{:S(2)}, u32[]{:S(2)}) collective-permute-start(f32[32,6,1,64]{3,0,2,1:T(8,128)S(1)} %get-tuple-element.16), channel_id=1, source_target_pairs={{1,0},{2,1},{3,2},{4,3},{5,4},{6,5},{7,6},{8,7},{9,8},{10,9},{11,1... | collective-permute-start | bytes 147464 | tf_op jit(solution)/shard_map/ppermute | solution.py:17
  277.1 5.5 collective-permute-start.10
  299.2 6.8 %copy-start.5 = (f32[8,8,1,136,16]{3,4,1,0,2:T(8,128)S(1)}, f32[8,8,1,136,16]{3,4,1,0,2:T(8,128)}, u32[]{:S(2)}) copy-start(f32[8,8,1,136,16]{3,4,1,0,2:T(8,128)} %copy-done.4) | copy-start | bytes 1671172
  313.2 205.4 %copy-start.2 = (f32[16,4,2,4,2,64,2]{0,6,5,4,3,2,1:T(2,128)S(1)}, f32[16,4,2,4,2,64,2]{0,6,5,4,3,2,1:T(2,128)}, u32[]{:S(2)}) copy-start(f32[16,4,2,4,2,64,2]{0,6,5,4,3,2,1:T(2,128)} %broadcast_in_dim.39) | copy-start | bytes 1572868
  313.2 205.4 %copy-start.3 = (f32[8,8,1,136,16]{4,3,1,0,2:T(8,128)S(1)}, f32[8,8,1,136,16]{4,3,1,0,2:T(8,128)}, u32[]{:S(2)}) copy-start(f32[8,8,1,136,16]{4,3,1,0,2:T(8,128)} %reshape.201) | copy-start | bytes 1671172
  518.6 81.7 %copy-start.1 = (f32[32,16,3,3,3]{0,1,4,3,2:T(8,128)S(1)}, f32[32,16,3,3,3]{0,1,4,3,2:T(8,128)}, u32[]{:S(2)}) copy-start(f32[32,16,3,3,3]{0,1,4,3,2:T(8,128)} %param.9) | copy-start | bytes 165892
  (5 other events, 15.6 us)
where the time goes:
time: 606 us; the launch traced here: 601 us
  matrix products  357 us (59%)
  blocking collectives  96.7 us (16%)
  local copies, waits for them, and re-layouts  83.1 us (14%)
  starting transfers between devices  35.4 us (6%)
  other arithmetic  22.9 us (4%)
    transpose x2, matrix products, kernel_grad(): return jnp.transpose(result, (1, 0, 2, 3, 4))  236 us
    conv_general_dilated x3, matrix products, convolve(): lax.conv_general_dilated(field[None], kernel, (1, 1, 1), padding, dimensi...  121 us
    psum x1, blocking collectives, on_device(): lax.psum((grad_kernel_one, grad_bias_one, grad_kernel_two, grad_bias_two)...  80.5 us
    conv_general_dilated x16, local copies, waits for them, and re-layouts, convolve(): lax.conv_general_dilated(field[None], kernel, (1, 1, 1), padding, dimensi...  27.1 us
    ppermute x6, starting transfers between devices, padded(): lax.ppermute(lax.slice_in_dim(block, block.shape[dim] - width, None, axis...  21.8 us
    all_to_all x1, blocking collectives, on_device(): lax.all_to_all(cotangent, 'gy', split_axis=2, concat_axis=0, tiled=True)  16.2 us
    mul x3, local copies, waits for them, and re-layouts, silu_slope(): return sigmoid_vals * (1.0 + act * (1.0 - sigmoid_vals))  13.5 us
  transfers between devices with their start and end apart: 13, of which 2 were waited for; matrix products, arithmetic and copies ran while one was open for 10% of the time, Pallas kernels for 0%

commit v1 on v0

v1 whole, which is shorter than its diff:
```python
import functools

import jax
import jax.numpy as jnp
from jax import lax
from jax.experimental import pallas as pl
from jax.experimental.pallas import tpu as pltpu
from jax.sharding import PartitionSpec as P

F32, BF16 = jnp.float32, jnp.bfloat16
HALO = 3
TAPS = [(a, b) for a in range(3) for b in range(3)]
NT = (((1,), (1,)), ((), ()))
VMEM = pltpu.CompilerParams(vmem_limit_bytes=56 * 2**20)


def mm(left, right):
    return jnp.dot(left, right, preferred_element_type=F32)


def mm_nt(left, right):
    return lax.dot_general(left, right, NT, preferred_element_type=F32)


def split2(value):
    high = value.astype(BF16)
    return high, (value - high.astype(F32)).astype(BF16)


def split3(value):
    high, rest = split2(value)
    low = value - high.astype(F32) - rest.astype(F32)
    return high, rest, low.astype(BF16)


def iota(shape, dim):
    return lax.broadcasted_iota(jnp.int32, shape, dim)


def lane_shift(value, by):
    axis = value.ndim - 1
    lane = iota(value.shape, axis)
    moved = pltpu.roll(value, by % 128, axis)
    keep = lane >= by if by > 0 else lane < 128 + by
    return jnp.where(keep, moved, 0.0)


def sigmoid(value):
    return 1.0 / (1.0 + jnp.exp(-value))


def eye(size):
    return (iota((size, size), 0) == iota((size, size), 1)).astype(BF16)


def xor_rows(value, bits, rows_per):
    rows = value.shape[0]
    group = iota(value.shape, 0) // rows_per
    for bit in range(4):
        span = rows_per << bit
        upper = (group >> bit) & 1
        swapped = jnp.where(
            upper == 1,
            pltpu.roll(value, span, 0),
            pltpu.roll(value, rows - span, 0),
        )
        value = jnp.where(((bits >> bit) & 1) == 1, swapped, value)
    return value


def prepare(k1, b1, k2, b2, left_one, left_two, left_back):
    def ones_first(bias, rows):
        row = iota((rows, bias.shape[1]), 0)
        return jnp.where(row == 0, jnp.broadcast_to(bias, (rows, bias.shape[1])), 0.0)

    taps = [jnp.concatenate([k1[t], k1[t]], axis=0) for t in range(27)]
    whole = jnp.concatenate(taps + [ones_first(b1[...], 8)], axis=0)
    high, low = split2(whole)
    left_one[0:16, :] = mm_nt(eye(16), high).astype(BF16)
    left_one[16:32, :] = mm_nt(eye(16), low).astype(BF16)
    taps = [jnp.concatenate([k2[t], k2[t]], axis=0) for t in range(27)]
    whole = jnp.concatenate(taps + [ones_first(b2[...], 16)], axis=0)
    high, low = split2(whole)
    left_two[0:32, :] = mm_nt(eye(32), high).astype(BF16)
    left_two[32:64, :] = mm_nt(eye(32), low).astype(BF16)
    for t in range(27):
        high, low = split2(k2[t])
        left_back[16 * t : 16 * t + 16, :] = jnp.concatenate([high, high, low, low], axis=1)


def work(
    place, edge, xlo, own, xhi, ylo, yhi, left_one, left_two, left_back, up,
    map_out, sums,
    s_one, p_one, d_one, s_two, p_two, d_two, y_back, g_one,
):
    scale_up = edge[12]

    def columns(block, x, y):
        high = block.astype(BF16).astype(F32)
        both = jnp.concatenate([high, block - high], axis=1)
        count = block.shape[0]
        s_one[x, y : y + count, 0:8, :] = lane_shift(both, 1)
        s_one[x, y : y + count, 8:16, :] = both
        s_one[x, y : y + count, 16:24, :] = lane_shift(both, -1)

    for ref, start in ((xlo, 0), (own, HALO), (xhi, HALO + own.shape[0])):
        for x in range(ref.shape[0]):
            columns(ref[x], start + x, HALO)
    for x in range(14):
        columns(ylo[x], x, 0)
        columns(yhi[x], x, 11)

    one_row = (iota((8, 128), 0) == 0).astype(F32)
    even = (iota((16, 128), 1) & 1) == 0

    def first(px, carry):
        total = None
        for dx in range(2):
            x = 2 * px + dx
            for y in range(12):
                patch = jnp.concatenate([s_one[x + a, y + b] for a, b in TAPS] + [one_row], axis=0)
                at = pl.multiple_of((x * 12 + y) * 128, 128)
                p_one[:, pl.ds(at, 128)] = patch.astype(BF16)
            at = pl.multiple_of(x * 1536, 1536)
            act = mm(left_one[...], p_one[:, pl.ds(at, 1536)])
            act = act[0:16] + act[16:32]
            gate = sigmoid(act)
            d_one[x] = gate * (1.0 + act * (1.0 - gate))
            total = act * gate if total is None else total + act * gate
        for py in range(6):
            at = 256 * py
            cell = total[:, at : at + 128] + total[:, at + 128 : at + 256]
            cell = cell + pltpu.roll(cell, 127, 1)
            cell = jnp.where(even, cell, 0.0) * (0.125 * edge[px] * edge[6 + py])
            for c, by in enumerate((2, 0, -2)):
                moved = lane_shift(cell, by) if by else cell
                high, low = split2(moved)
                s_two[px, py, 32 * c : 32 * c + 32, :] = jnp.concatenate([high, low], axis=0)
        return carry

    lax.fori_loop(0, 6, first, 0)

    ones_rows = (iota((16, 128), 0) == 0).astype(F32).astype(BF16)
    cells = []
    for x in range(4):
        for y in range(4):
            at = (x * 4 + y) * 128
            for t, (a, b) in enumerate(TAPS):
                p_two[96 * t : 96 * t + 96, at : at + 128] = s_two[x + a, y + b]
            p_two[864:880, at : at + 128] = ones_rows
        act = mm(left_two[...], p_two[:, 512 * x : 512 * x + 512])
        act = act[0:32] + act[32:64]
        gate = sigmoid(act)
        d_two[x] = gate * (1.0 + act * (1.0 - gate))
        value = act * gate
        total = value if x % 2 == 0 else total + value
        if x % 2 == 1:
            for my in range(2):
                cell = total[:, 256 * my : 256 * my + 128] + total[:, 256 * my + 128 : 256 * my + 256]
                cells.append((cell + pltpu.roll(cell, 126, 1)) * 0.125)
    quad = jnp.concatenate(cells, axis=1)
    row, col = iota((512, 128), 0), iota((512, 128), 1)
    pick = ((row >> 7) == (col >> 5)) & ((row & 127) == 4 * (col & 31))
    parts = mm(jnp.concatenate(split3(quad), axis=0), pick.astype(F32).astype(BF16))
    map_out[...] = xor_rows(parts[0:32] + parts[32:64] + parts[64:96], place[0], 2)

    row, col = iota((128, 512), 0), iota((128, 512), 1)
    pick = ((row >> 5) == (col >> 7)) & ((row & 31) == ((col & 127) >> 2)) & ((col & 1) == 0)
    parts = mm(jnp.concatenate(split3(up[...]), axis=0), pick.astype(F32).astype(BF16))
    wide = (parts[0:32] + parts[32:64] + parts[64:96]) * (0.125 * scale_up)
    highs, lows = [], []
    for x in range(4):
        for y in range(4):
            at = ((x // 2) * 2 + y // 2) * 128
            high, low = split2(wide[:, at : at + 128] * d_two[x, :, 128 * y : 128 * y + 128])
            highs.append(high)
            lows.append(low)
    high, low = jnp.concatenate(highs, axis=1), jnp.concatenate(lows, axis=1)
    grad_two = jnp.concatenate([high, low], axis=0)

    y_back[...] = mm(left_back[...], jnp.concatenate([grad_two, grad_two], axis=0))

    found = mm_nt(p_two[...], grad_two)
    found = found + pltpu.roll(jnp.concatenate([found, found], axis=1), 96, 1)[:, 0:64]
    groups = [found[32 * t : 32 * t + 16] + found[32 * t + 16 : 32 * t + 32] for t in range(27)]
    groups.append(found[864:880])
    slots = [jnp.concatenate(groups[7 * s : 7 * s + 7], axis=0)[:, 0:32] for s in range(4)]
    sums[0:112, :] = jnp.concatenate(slots, axis=1)

    for px in range(6):
        for py in range(6):
            acc = [None] * 3
            for a, b in TAPS:
                x, y = px - a, py - b
                if not (0 <= x < 4 and 0 <= y < 4):
                    continue
                at = (x * 4 + y) * 128
                for c in range(3):
                    start = ((a * 3 + b) * 3 + c) * 16
                    block = y_back[start : start + 16, at : at + 128]
                    acc[c] = block if acc[c] is None else acc[c] + block
            cell = acc[1] + lane_shift(acc[0], -2) + lane_shift(acc[2], 2)
            cell = (cell + pltpu.roll(cell, 1, 1)) * (0.125 * edge[px] * edge[6 + py])
            for dx in range(2):
                for dy in range(2):
                    x, y = 2 * px + dx, 2 * py + dy
                    high, low = split2(cell * d_one[x, :, 128 * y : 128 * y + 128])
                    at = (x * 12 + y) * 128
                    g_one[:, at : at + 128] = jnp.concatenate([high, low], axis=0)

    def last(step, total):
        at = pl.multiple_of(step * 3072, 3072)
        return total + mm_nt(p_one[:, pl.ds(at, 3072)], g_one[:, pl.ds(at, 3072)])

    found = lax.fori_loop(0, 6, last, jnp.zeros((224, 32), F32))
    found = (found[:, 0:16] + found[:, 16:32]).reshape(28, 8, 16)
    upper = jnp.concatenate([found[:, 4:8], found[:, 0:4]], axis=1)
    found = found + upper
    blank = jnp.zeros((8, 16), F32)
    blocks = [found[g] for g in range(28)] + [blank] * 4
    strips = [jnp.concatenate(blocks[8 * t : 8 * t + 8], axis=1) for t in range(4)]
    low_rows = iota((8, 128), 0) < 4
    sums[112:120, :] = jnp.where(low_rows, strips[0], strips[1])
    sums[120:128, :] = jnp.where(low_rows, strips[2], strips[3])


def finish(place, sums, other, mine, pooled, gk1, gb1, gk2, gb2):
    total = sums[...] + other[...]
    for g in range(27):
        s, t = g // 7, g % 7
        gk2[g] = total[16 * t : 16 * t + 16, 32 * s : 32 * s + 32]
    gb2[...] = total[96:97, 96:128]
    for g in range(27):
        t, s = g // 8, g % 8
        start = 112 + 8 * (t // 2) + 4 * (t % 2)
        gk1[g] = total[start : start + 4, 16 * s : 16 * s + 16]
    gb1[...] = total[124:125, 48:64]
    pooled[...] = xor_rows(mine[...], place[0], 2)


def shift_pairs(count, step):
    return [(i, i + step) for i in range(count) if 0 <= i + step < count]


def neighbours(block, axis, dim):
    count = lax.axis_size(axis)
    size = block.shape[dim]
    low = lax.slice_in_dim(block, size - HALO, size, axis=dim)
    high = lax.slice_in_dim(block, 0, HALO, axis=dim)
    return (
        lax.ppermute(low, axis, shift_pairs(count, 1)),
        lax.ppermute(high, axis, shift_pairs(count, -1)),
    )


def call(kernel, outs, ins, scratch=()):
    return pl.pallas_call(
        kernel,
        out_shape=[jax.ShapeDtypeStruct(*o) for o in outs],
        in_specs=[pl.BlockSpec(memory_space=m) for m in ins],
        out_specs=[pl.BlockSpec(memory_space=pltpu.VMEM) for _ in outs],
        scratch_shapes=list(scratch),
        compiler_params=VMEM,
    )


def on_device(volume, kernel_one, bias_one, kernel_two, bias_two, cotangent):
    gx, gy = lax.axis_index("gx"), lax.axis_index("gy")
    nx, ny = lax.axis_size("gx"), lax.axis_size("gy")
    vm, sm = pltpu.VMEM, pltpu.SMEM

    own = jnp.transpose(volume, (1, 2, 0, 3))
    xlo, xhi = neighbours(own, "gx", 0)
    full = jnp.concatenate([xlo, own, xhi], axis=0)
    ylo, yhi = neighbours(full, "gy", 1)

    send = jnp.transpose(cotangent.reshape(2, 2, 16, 64), (2, 0, 1, 3)).reshape(32, 128)
    up = lax.all_to_all(send, "gy", 0, 0, tiled=True)

    k1 = jnp.transpose(kernel_one, (2, 3, 4, 1, 0)).reshape(27, 4, 16)
    k2 = jnp.transpose(kernel_two, (2, 3, 4, 1, 0)).reshape(27, 16, 32)
    left_one, left_two, left_back = call(
        prepare, [((32, 224), BF16), ((64, 880), BF16), ((432, 128), BF16)], [vm] * 4
    )(k1, bias_one[None], k2, bias_two[None])

    inside = lambda at, size, n: jnp.where(
        ((at == 0) & (jnp.arange(6) == 0)) | ((at == n - 1) & (jnp.arange(6) == 5)), 0.0, 1.0
    )
    scale = 8.0 / (volume.shape[1] * nx)
    edge = jnp.concatenate(
        [inside(gx, 6, nx), inside(gy, 6, ny), jnp.full((4,), scale)]
    ).astype(F32)
    place = gy.astype(jnp.int32).reshape(1)

    mapped, sums = call(
        work,
        [((32, 128), F32), ((128, 128), F32)],
        [sm, sm] + [vm] * 9,
        [
            pltpu.VMEM((14, 14, 24, 128), F32),
            pltpu.VMEM((224, 18432), BF16),
            pltpu.VMEM((12, 16, 1536), F32),
            pltpu.VMEM((6, 6, 96, 128), BF16),
            pltpu.VMEM((880, 2048), BF16),
            pltpu.VMEM((4, 32, 512), F32),
            pltpu.VMEM((432, 2048), F32),
            pltpu.VMEM((32, 18432), BF16),
        ],
    )(place, edge, xlo, own, xhi, ylo, yhi, left_one, left_two, left_back, up)

    slots = mapped.reshape(2, 2, 2, 2, 2, 128)
    for bit in range(4):
        dim = 3 - bit
        kept, sent = (lax.index_in_dim(slots, k, dim, keepdims=True) for k in range(2))
        packed = jnp.concatenate([sums, sent.reshape(16, 128)], axis=0)
        got = lax.ppermute(packed, "gy", [(i, i ^ (1 << bit)) for i in range(16)])
        sums = sums + got[0:128]
        slots = jnp.concatenate([kept, got[128:144].reshape(sent.shape)], axis=dim)
    for bit in range(3):
        got = lax.ppermute(sums, "gx", [(i, i ^ (1 << bit)) for i in range(8)])
        if bit < 2:
            sums = sums + got

    pooled, gk1, gb1, gk2, gb2 = call(
        finish,
        [((32, 128), F32), ((27, 4, 16), F32), ((1, 16), F32), ((27, 16, 32), F32), ((1, 32), F32)],
        [sm] + [vm] * 3,
    )(place, sums, got, slots.reshape(32, 128))
    pooled = jnp.transpose(pooled.reshape(16, 2, 2, 64), (1, 2, 0, 3)).reshape(2, 2, 1024)
    gk1 = jnp.transpose(gk1.reshape(3, 3, 3, 4, 16), (4, 3, 0, 1, 2))
    gk2 = jnp.transpose(gk2.reshape(3, 3, 3, 16, 32), (4, 3, 0, 1, 2))
    return (pooled, gk1, gb1[0], gk2, gb2[0])


def solution(mesh):
    in_specs = (P(None, "gx", "gy", None), P(), P(), P(), P(), P("gy", "gx", None))
    out_specs = (P("gy", "gx", None), P(), P(), P(), P())
    return jax.shard_map(
        on_device, mesh=mesh, in_specs=in_specs, out_specs=out_specs, check_vma=False
    )
```

time: 606 us -> 87.4 us (0.14)
  the two profiles are of different devices: /device:TPU:0 before, /device:TPU:38 now
where the time goes in v1:
time: 87.4 us; the launch traced here: 86.9 us
  waiting for transfers between devices  39.6 us (45%)
  starting transfers between devices  21.5 us (25%)
  Pallas kernels  16.8 us (19%)
  local copies, waits for them, and re-layouts  5.7 us (7%)
  other arithmetic  2.28 us (3%)
  between operations  0.94 us (1%)
    ppermute x4, waiting for transfers between devices, on_device(): got = lax.ppermute(packed, 'gy', [(i, i ^ 1 << bit) for i in range(16)])  16.2 us
    ppermute x3, waiting for transfers between devices, on_device(): got = lax.ppermute(sums, 'gx', [(i, i ^ 1 << bit) for i in range(8)])  13.6 us
    pallas_call x1, Pallas kernels, on_device(): call(work, [((32, 128), F32), ((128, 128), F32)], [sm, sm] + [vm] * 9, [p...  13.2 us
    ppermute x2, waiting for transfers between devices, neighbours(): lax.ppermute(low, axis, shift_pairs(count, 1))  9.78 us
    ppermute x2, starting transfers between devices, neighbours(): lax.ppermute(high, axis, shift_pairs(count, -1))  8.24 us
    all_to_all x1, starting transfers between devices, on_device(): up = lax.all_to_all(send, 'gy', 0, 0, tiled=True)  7.21 us
    ppermute x2, starting transfers between devices, neighbours(): lax.ppermute(low, axis, shift_pairs(count, 1))  3.84 us
    pallas_call x1, Pallas kernels, on_device(): call(prepare, [((32, 224), BF16), ((64, 880), BF16), ((432, 128), BF16)],...  2 us
  transfers between devices with their start and end apart: 12, of which 9 were waited for; matrix products, arithmetic and copies ran while one was open for 2% of the time, Pallas kernels for 2%

profile of v1, /device:TPU:38, one launch (start us, length us, event | category | flops | bytes accessed | tf_op | source)
XLA Modules:
  0.0 86.9 jit_solution(12180032339442880286)
XLA Ops:
  0.6 0.8 reshape.71
  1.5 0.7 all_to_all.7
  2.2 7.2 %all-to-all-start = ((f32[16,2,128]{2,1,0:T(2,128)}), f32[16,2,128]{2,1,0:T(2,128)S(1)}, u32[]{:S(2)}, u32[]{:S(2)}) async-start(f32[16,2,128]{2,1,0:T(2,128)} %all_to_all.7), calls=%async_computation | async-start | bytes 32768 | tf_op jit(solution)/shard_map/all_to_all | solution.py:278
  9.5 5.4 %collective-permute-start.1 = (f32[3,8,4,128]{3,2,1,0:T(4,128)S(1)}, f32[3,8,4,128]{3,2,1,0:T(4,128)S(1)}, u32[]{:S(2)}, u32[]{:S(2)}) collective-permute-start(f32[3,8,4,128]{3,2,1,0:T(4,128)S(1)} %get-tuple-element.27), channel_id=1, source_target_pairs={{16,0},{32,16},{48,32},{64,48},{80,64},{96,80},{112,96},{17,1},{33... | collective-permute-start | bytes 147464 | tf_op jit(solution)/shard_map/ppermute | solution.py:252
  14.9 1.9 %collective-permute-start = (f32[3,8,4,128]{3,2,1,0:T(4,128)S(1)}, f32[3,8,4,128]{3,2,1,0:T(4,128)S(1)}, u32[]{:S(2)}, u32[]{:S(2)}) collective-permute-start(f32[3,8,4,128]{3,2,1,0:T(4,128)S(1)} %get-tuple-element.28), channel_id=1, source_target_pairs={{0,16},{16,32},{32,48},{48,64},{64,80},{80,96},{96,112},{1,17},{17... | collective-permute-start | bytes 147464 | tf_op jit(solution)/shard_map/ppermute | solution.py:251
  16.9 6.1 %collective-permute-done.xlo = f32[3,8,4,128]{3,2,1,0:T(4,128)S(1)} collective-permute-done((f32[3,8,4,128]{3,2,1,0:T(4,128)S(1)}, f32[3,8,4,128]{3,2,1,0:T(4,128)S(1)}, u32[]{:S(2)}, u32[]{:S(2)}) %collective-permute-start) | collective-permute-done | bytes 49184 | tf_op jit(solution)/shard_map/ppermute | solution.py:251
  23.6 2.9 %collective-permute-start.3 = (f32[14,3,4,128]{3,2,1,0:T(4,128)S(1)}, f32[14,3,4,128]{3,2,1,0:T(4,128)S(1)}, u32[]{:S(2)}, u32[]{:S(2)}) collective-permute-start(f32[14,3,4,128]{3,2,1,0:T(4,128)S(1)} %get-tuple-element.25), channel_id=1, source_target_pairs={{1,0},{2,1},{3,2},{4,3},{5,4},{6,5},{7,6},{8,7},{9,8},{10,9},{11,1... | collective-permute-start | bytes 258056 | tf_op jit(solution)/shard_map/ppermute | solution.py:252
  26.5 1.9 %collective-permute-start.2 = (f32[14,3,4,128]{3,2,1,0:T(4,128)S(1)}, f32[14,3,4,128]{3,2,1,0:T(4,128)S(1)}, u32[]{:S(2)}, u32[]{:S(2)}) collective-permute-start(f32[14,3,4,128]{3,2,1,0:T(4,128)S(1)} %get-tuple-element.26), channel_id=1, source_target_pairs={{0,1},{1,2},{2,3},{3,4},{4,5},{5,6},{6,7},{7,8},{8,9},{9,10},{10,1... | collective-permute-start | bytes 258056 | tf_op jit(solution)/shard_map/ppermute | solution.py:251
  29.0 2.0 %shard_map.101 = (bf16[32,224]{1,0:T(8,128)(2,1)}, bf16[64,880]{1,0:T(8,128)(2,1)}, bf16[432,128]{1,0:T(8,128)(2,1)}) custom-call(f32[27,4,16]{2,1,0:T(4,128)} %bitcast.54, f32[1,16]{1,0:T(1,128)} %bitcast.61, f32[27,16,32]{2,1,0:T(8,128)} %bitcast.44, f32[1,32]{1,0:T(1,128)} %bitcast.62), custom_call_target="tpu_custom_call" | custom-call | tf_op jit(solution)/shard_map/pallas_call | solution.py:282
  31.1 3.7 %collective-permute-done.2.ylo = f32[14,3,4,128]{3,2,1,0:T(4,128)S(1)} collective-permute-done((f32[14,3,4,128]{3,2,1,0:T(4,128)S(1)}, f32[14,3,4,128]{3,2,1,0:T(4,128)S(1)}, u32[]{:S(2)}, u32[]{:S(2)}) %collective-permute-start.2) | collective-permute-done | bytes 86048 | tf_op jit(solution)/shard_map/ppermute | solution.py:251
  35.3 13.2 %shard_map.102 = (f32[32,128]{1,0:T(8,128)}, f32[128,128]{1,0:T(8,128)}) custom-call(s32[1]{0:T(128)} %bitcast.place, f32[16]{0:T(128)} %pad_maximum_fusion.7.edge, f32[3,8,4,128]{3,2,1,0:T(4,128)} %copy-done.4, f32[8,8,4,128]{3,2,1,0:T(4,128)} %bitcast.43, f32[3,8,4,128]{3,2,1,0:T(4,128)} %copy-done.3, f32[14,3,4,128]{3,2,1,0:T(4,128)} %copy-done.7, ...), custom_call_target="tpu_custom_call" | custom-call | tf_op jit(solution)/shard_map/pallas_call | solution.py:295
  48.5 0.7 fusion.8
  49.2 0.9 %pad_maximum_fusion.3 = f32[144,128]{1,0:T(8,128)S(1)} fusion(f32[16,128]{1,0:T(8,128)S(1)} %bitcast.59, f32[128,128]{1,0:T(8,128)} %get-tuple-element.18), kind=kLoop, calls=%fused_computation.4 | loop fusion | flops 18432 | bytes 147456 | tf_op jit(solution)/shard_map/concatenate | solution.py:315
  50.1 1.3 %collective-permute-done.4 = f32[144,128]{1,0:T(8,128)S(1)} collective-permute-done((f32[144,128]{1,0:T(8,128)S(1)}, f32[144,128]{1,0:T(8,128)S(1)}, u32[]{:S(2)}, u32[]{:S(2)}) %collective-permute-start.4) | collective-permute-done | bytes 73760 | tf_op jit(solution)/shard_map/ppermute | solution.py:316
  51.5 0.7 collective-permute-start.5
  52.1 5.3 %collective-permute-done.5 = f32[144,128]{1,0:T(8,128)S(1)} collective-permute-done((f32[144,128]{1,0:T(8,128)S(1)}, f32[144,128]{1,0:T(8,128)S(1)}, u32[]{:S(2)}, u32[]{:S(2)}) %collective-permute-start.5) | collective-permute-done | bytes 73760 | tf_op jit(solution)/shard_map/ppermute | solution.py:316
  58.1 4.4 %collective-permute-done.6 = f32[144,128]{1,0:T(8,128)S(1)} collective-permute-done((f32[144,128]{1,0:T(8,128)S(1)}, f32[144,128]{1,0:T(8,128)S(1)}, u32[]{:S(2)}, u32[]{:S(2)}) %collective-permute-start.6) | collective-permute-done | bytes 73760 | tf_op jit(solution)/shard_map/ppermute | solution.py:316
  63.2 5.3 %collective-permute-done.7 = f32[144,128]{1,0:T(8,128)S(1)} collective-permute-done((f32[144,128]{1,0:T(8,128)S(1)}, f32[144,128]{1,0:T(8,128)S(1)}, u32[]{:S(2)}, u32[]{:S(2)}) %collective-permute-start.7) | collective-permute-done | bytes 73760 | tf_op jit(solution)/shard_map/ppermute | solution.py:316
  68.6 4.3 %collective-permute-done.8 = f32[128,128]{1,0:T(8,128)S(1)} collective-permute-done((f32[128,128]{1,0:T(8,128)S(1)}, f32[128,128]{1,0:T(8,128)S(1)}, u32[]{:S(2)}, u32[]{:S(2)}) %collective-permute-start.8) | collective-permute-done | bytes 65568 | tf_op jit(solution)/shard_map/ppermute | solution.py:320
  73.0 5.7 %collective-permute-done.9 = f32[128,128]{1,0:T(8,128)S(1)} collective-permute-done((f32[128,128]{1,0:T(8,128)S(1)}, f32[128,128]{1,0:T(8,128)S(1)}, u32[]{:S(2)}, u32[]{:S(2)}) %collective-permute-start.9) | collective-permute-done | bytes 65568 | tf_op jit(solution)/shard_map/ppermute | solution.py:320
  79.4 3.6 %collective-permute-done.10.other = f32[128,128]{1,0:T(8,128)S(1)} collective-permute-done((f32[128,128]{1,0:T(8,128)S(1)}, f32[128,128]{1,0:T(8,128)S(1)}, u32[]{:S(2)}, u32[]{:S(2)}) %collective-permute-start.10) | collective-permute-done | bytes 65568 | tf_op jit(solution)/shard_map/ppermute | solution.py:320
  83.7 1.7 %shard_map.103 = (f32[32,128]{1,0:T(8,128)}, f32[27,4,16]{2,1,0:T(4,128)}, f32[1,16]{1,0:T(1,128)}, f32[27,16,32]{2,1,0:T(8,128)}, f32[1,32]{1,0:T(1,128)}) custom-call(s32[1]{0:T(128)} %bitcast.place, f32[128,128]{1,0:T(8,128)} %copy-done.2, f32[128,128]{1,0:T(8,128)} %copy-done.10, f32[32,128]{1,0:T(8,128)} %bitcast.53), custom_call_target="tpu_custom_call" | custom-call | tf_op jit(solution)/shard_map/pallas_call | solution.py:324
  85.4 0.8 reshape.82
  86.2 0.7 reshape.83
  (58 shorter events, 4.9 us)
Async XLA Ops:
  0.6 8.8 %copy-start.5 = (f32[4,8,8,128]{3,2,1,0:T(8,128)S(1)}, f32[4,8,8,128]{3,2,1,0:T(8,128)}, u32[]{:S(2)}) copy-start(f32[4,8,8,128]{3,2,1,0:T(8,128)} %param.6) | copy-start | bytes 393220
  2.2 28.8 %all-to-all-start = ((f32[16,2,128]{2,1,0:T(2,128)}), f32[16,2,128]{2,1,0:T(2,128)S(1)}, u32[]{:S(2)}, u32[]{:S(2)}) async-start(f32[16,2,128]{2,1,0:T(2,128)} %all_to_all.7), calls=%async_computation | async-start | bytes 32768 | tf_op jit(solution)/shard_map/all_to_all | solution.py:278
  9.5 13.5 %copy-start = (f32[4,8,8,128]{3,0,2,1:T(4,128)}, f32[4,8,8,128]{3,0,2,1:T(4,128)S(1)}, u32[]{:S(2)}) copy-start(f32[4,8,8,128]{3,0,2,1:T(4,128)S(1)} %copy.18) | copy-start | bytes 393220
  9.5 7.3 %collective-permute-start.1 = (f32[3,8,4,128]{3,2,1,0:T(4,128)S(1)}, f32[3,8,4,128]{3,2,1,0:T(4,128)S(1)}, u32[]{:S(2)}, u32[]{:S(2)}) collective-permute-start(f32[3,8,4,128]{3,2,1,0:T(4,128)S(1)} %get-tuple-element.27), channel_id=1, source_target_pairs={{16,0},{32,16},{48,32},{64,48},{80,64},{96,80},{112,96},{17,1},{33... | collective-permute-start | bytes 147464 | tf_op jit(solution)/shard_map/ppermute | solution.py:252
  14.9 8.1 %collective-permute-start = (f32[3,8,4,128]{3,2,1,0:T(4,128)S(1)}, f32[3,8,4,128]{3,2,1,0:T(4,128)S(1)}, u32[]{:S(2)}, u32[]{:S(2)}) collective-permute-start(f32[3,8,4,128]{3,2,1,0:T(4,128)S(1)} %get-tuple-element.28), channel_id=1, source_target_pairs={{0,16},{16,32},{32,48},{48,64},{64,80},{80,96},{96,112},{1,17},{17... | collective-permute-start | bytes 147464 | tf_op jit(solution)/shard_map/ppermute | solution.py:251
  16.9 6.2 %copy-start.3 = (f32[3,8,4,128]{3,2,1,0:T(4,128)}, f32[3,8,4,128]{3,2,1,0:T(4,128)S(1)}, u32[]{:S(2)}) copy-start(f32[3,8,4,128]{3,2,1,0:T(4,128)S(1)} %collective-permute-done.1.xhi) | copy-start | bytes 147460
  23.0 0.6 copy-start.4
  23.6 7.4 %collective-permute-start.3 = (f32[14,3,4,128]{3,2,1,0:T(4,128)S(1)}, f32[14,3,4,128]{3,2,1,0:T(4,128)S(1)}, u32[]{:S(2)}, u32[]{:S(2)}) collective-permute-start(f32[14,3,4,128]{3,2,1,0:T(4,128)S(1)} %get-tuple-element.25), channel_id=1, source_target_pairs={{1,0},{2,1},{3,2},{4,3},{5,4},{6,5},{7,6},{8,7},{9,8},{10,9},{11,1... | collective-permute-start | bytes 258056 | tf_op jit(solution)/shard_map/ppermute | solution.py:252
  26.5 8.2 %collective-permute-start.2 = (f32[14,3,4,128]{3,2,1,0:T(4,128)S(1)}, f32[14,3,4,128]{3,2,1,0:T(4,128)S(1)}, u32[]{:S(2)}, u32[]{:S(2)}) collective-permute-start(f32[14,3,4,128]{3,2,1,0:T(4,128)S(1)} %get-tuple-element.26), channel_id=1, source_target_pairs={{0,1},{1,2},{2,3},{3,4},{4,5},{5,6},{6,7},{7,8},{8,9},{9,10},{10,1... | collective-permute-start | bytes 258056 | tf_op jit(solution)/shard_map/ppermute | solution.py:251
  31.0 3.7 %copy-start.9 = (f32[16,2,128]{2,1,0:T(2,128)}, f32[16,2,128]{2,1,0:T(2,128)S(1)}, u32[]{:S(2)}) copy-start(f32[16,2,128]{2,1,0:T(2,128)S(1)} %all-to-all-done) | copy-start | bytes 49156
  31.0 3.7 %copy-start.6 = (f32[14,3,4,128]{3,2,1,0:T(4,128)}, f32[14,3,4,128]{3,2,1,0:T(4,128)S(1)}, u32[]{:S(2)}) copy-start(f32[14,3,4,128]{3,2,1,0:T(4,128)S(1)} %collective-permute-done.3.yhi) | copy-start | bytes 258052
  34.7 0.6 copy-start.7
  49.2 2.2 %copy-start.1 = (f32[128,128]{1,0:T(8,128)S(1)}, f32[128,128]{1,0:T(8,128)}, u32[]{:S(2)}) copy-start(f32[128,128]{1,0:T(8,128)} %get-tuple-element.18) | copy-start | bytes 196612
  50.1 1.3 %collective-permute-start.4 = (f32[144,128]{1,0:T(8,128)S(1)}, f32[144,128]{1,0:T(8,128)S(1)}, u32[]{:S(2)}, u32[]{:S(2)}) collective-permute-start(f32[144,128]{1,0:T(8,128)S(1)} %pad_maximum_fusion.3), channel_id=1, source_target_pairs={{0,1},{1,0},{2,3},{3,2},{4,5},{5,4},{6,7},{7,6},{8,9},{9,8},{10,11... | collective-permute-start | bytes 221192 | tf_op jit(solution)/shard_map/ppermute | solution.py:316
  51.5 5.9 %collective-permute-start.5 = (f32[144,128]{1,0:T(8,128)S(1)}, f32[144,128]{1,0:T(8,128)S(1)}, u32[]{:S(2)}, u32[]{:S(2)}) collective-permute-start(f32[144,128]{1,0:T(8,128)S(1)} %pad_maximum_fusion.4), channel_id=1, source_target_pairs={{0,2},{1,3},{2,0},{3,1},{4,6},{5,7},{6,4},{7,5},{8,10},{9,11},{10,... | collective-permute-start | bytes 221192 | tf_op jit(solution)/shard_map/ppermute | solution.py:316
  57.5 5.0 %collective-permute-start.6 = (f32[144,128]{1,0:T(8,128)S(1)}, f32[144,128]{1,0:T(8,128)S(1)}, u32[]{:S(2)}, u32[]{:S(2)}) collective-permute-start(f32[144,128]{1,0:T(8,128)S(1)} %pad_maximum_fusion.5), channel_id=1, source_target_pairs={{0,4},{1,5},{2,6},{3,7},{4,0},{5,1},{6,2},{7,3},{8,12},{9,13},{10,... | collective-permute-start | bytes 221192 | tf_op jit(solution)/shard_map/ppermute | solution.py:316
  62.5 5.9 %collective-permute-start.7 = (f32[144,128]{1,0:T(8,128)S(1)}, f32[144,128]{1,0:T(8,128)S(1)}, u32[]{:S(2)}, u32[]{:S(2)}) collective-permute-start(f32[144,128]{1,0:T(8,128)S(1)} %pad_maximum_fusion.6), channel_id=1, source_target_pairs={{0,8},{1,9},{2,10},{3,11},{4,12},{5,13},{6,14},{7,15},{8,0},{9,1},... | collective-permute-start | bytes 221192 | tf_op jit(solution)/shard_map/ppermute | solution.py:316
  68.5 4.5 %copy-start.8 = (f32[144,128]{1,0:T(8,128)}, f32[144,128]{1,0:T(8,128)S(1)}, u32[]{:S(2)}) copy-start(f32[144,128]{1,0:T(8,128)S(1)} %collective-permute-done.7) | copy-start | bytes 221188
  68.5 4.3 %collective-permute-start.8 = (f32[128,128]{1,0:T(8,128)S(1)}, f32[128,128]{1,0:T(8,128)S(1)}, u32[]{:S(2)}, u32[]{:S(2)}) collective-permute-start(f32[128,128]{1,0:T(8,128)S(1)} %slice_add_fusion), channel_id=1, source_target_pairs={{0,16},{16,0},{32,48},{48,32},{64,80},{80,64},{96,112},{112,96},{1... | collective-permute-start | bytes 196616 | tf_op jit(solution)/shard_map/ppermute | solution.py:320
  72.9 5.8 %collective-permute-start.9 = (f32[128,128]{1,0:T(8,128)S(1)}, f32[128,128]{1,0:T(8,128)S(1)}, u32[]{:S(2)}, u32[]{:S(2)}) collective-permute-start(f32[128,128]{1,0:T(8,128)S(1)} %add.22), channel_id=1, source_target_pairs={{0,32},{16,48},{32,0},{48,16},{64,96},{80,112},{96,64},{112,80},{1... | collective-permute-start | bytes 196616 | tf_op jit(solution)/shard_map/ppermute | solution.py:320
  73.0 5.9 %slice-start = ((f32[144,128]{1,0:T(8,128)}), f32[16,128]{1,0:T(8,128)S(1)}, s32[]{:S(2)}) async-start(f32[144,128]{1,0:T(8,128)} %copy-done.8), calls=%async_computation.1 | async-start | bytes 16384 | tf_op jit(solution)/shard_map/slice | solution.py:318
  78.7 4.4 %copy-start.2 = (f32[128,128]{1,0:T(8,128)}, f32[128,128]{1,0:T(8,128)S(1)}, u32[]{:S(2)}) copy-start(f32[128,128]{1,0:T(8,128)S(1)} %add.23.sums) | copy-start | bytes 196612
  78.7 4.3 %collective-permute-start.10 = (f32[128,128]{1,0:T(8,128)S(1)}, f32[128,128]{1,0:T(8,128)S(1)}, u32[]{:S(2)}, u32[]{:S(2)}) collective-permute-start(f32[128,128]{1,0:T(8,128)S(1)} %add.23.sums), channel_id=1, source_target_pairs={{0,64},{16,80},{32,96},{48,112},{64,0},{80,16},{96,32},{112,48},{1... | collective-permute-start | bytes 196616 | tf_op jit(solution)/shard_map/ppermute | solution.py:320
  83.1 0.6 copy-start.10

commit v2 on v1

--- a/solution.py
+++ b/solution.py
@@ -11,7 +11,6 @@
 HALO = 3
 TAPS = [(a, b) for a in range(3) for b in range(3)]
 NT = (((1,), (1,)), ((), ()))
-VMEM = pltpu.CompilerParams(vmem_limit_bytes=56 * 2**20)
 
 
 def mm(left, right):
@@ -68,10 +67,33 @@
     return value
 
 
-def prepare(k1, b1, k2, b2, left_one, left_two, left_back):
+def prepare(
+    place, k1_hbm, b1_hbm, k2_hbm, b2_hbm, cot_hbm, left_one, left_two, left_back, send,
+    k1, b1, k2, b2, cot, sems,
+):
+    moves = [
+        pltpu.make_async_copy(source, target, sems.at[i])
+        for i, (source, target) in enumerate(
+            ((k1_hbm, k1), (b1_hbm, b1), (k2_hbm, k2), (b2_hbm, b2), (cot_hbm, cot))
+        )
+    ]
+    for move in moves:
+        move.start()
+    for move in moves:
+        move.wait()
+
     def ones_first(bias, rows):
         row = iota((rows, bias.shape[1]), 0)
         return jnp.where(row == 0, jnp.broadcast_to(bias, (rows, bias.shape[1])), 0.0)
+
+    lower = iota((1, 128), 1) < 64
+    rows = [None] * 32
+    for f in range(2):
+        for k in range(8):
+            near, far = (cot[f, m : m + 1, 128 * k : 128 * k + 128] for m in range(2))
+            rows[4 * k + f] = jnp.where(lower, near, pltpu.roll(far, 64, 1))
+            rows[4 * k + 2 + f] = jnp.where(lower, pltpu.roll(near, 64, 1), far)
+    send[...] = swap_last(xor_rows(jnp.concatenate(rows, axis=0), place[0], 2))
 
     taps = [jnp.concatenate([k1[t], k1[t]], axis=0) for t in range(27)]
     whole = jnp.concatenate(taps + [ones_first(b1[...], 8)], axis=0)
@@ -88,41 +110,34 @@
         left_back[16 * t : 16 * t + 16, :] = jnp.concatenate([high, high, low, low], axis=1)
 
 
-def work(
-    place, edge, xlo, own, xhi, ylo, yhi, left_one, left_two, left_back, up,
-    map_out, sums,
-    s_one, p_one, d_one, s_two, p_two, d_two, y_back, g_one,
+def columns(block):
+    high = block.astype(BF16).astype(F32)
+    both = jnp.concatenate([high, block - high], axis=1)
+    return jnp.concatenate([lane_shift(both, 1), both, lane_shift(both, -1)], axis=1)
+
+
+def forward(
+    place, edge, xlo, own, xhi, ylo, yhi, left_one, left_two, unused,
+    p_one, d_one, p_two, d_two, map_out,
+    s_one, s_two,
 ):
-    scale_up = edge[12]
-
-    def columns(block, x, y):
-        high = block.astype(BF16).astype(F32)
-        both = jnp.concatenate([high, block - high], axis=1)
-        count = block.shape[0]
-        s_one[x, y : y + count, 0:8, :] = lane_shift(both, 1)
-        s_one[x, y : y + count, 8:16, :] = both
-        s_one[x, y : y + count, 16:24, :] = lane_shift(both, -1)
-
     for ref, start in ((xlo, 0), (own, HALO), (xhi, HALO + own.shape[0])):
         for x in range(ref.shape[0]):
-            columns(ref[x], start + x, HALO)
+            s_one[start + x, 3:11] = columns(ref[x])
     for x in range(14):
-        columns(ylo[x], x, 0)
-        columns(yhi[x], x, 11)
-
+        s_one[x, 0:3] = columns(ylo[x])
+        s_one[x, 11:14] = columns(yhi[x])
+    even = (iota((16, 128), 1) & 1) == 0
     one_row = (iota((8, 128), 0) == 0).astype(F32)
-    even = (iota((16, 128), 1) & 1) == 0
-
-    def first(px, carry):
+
+    for px in range(6):
         total = None
-        for dx in range(2):
-            x = 2 * px + dx
+        for x in (2 * px, 2 * px + 1):
+            at = 1536 * x
             for y in range(12):
                 patch = jnp.concatenate([s_one[x + a, y + b] for a, b in TAPS] + [one_row], axis=0)
-                at = pl.multiple_of((x * 12 + y) * 128, 128)
-                p_one[:, pl.ds(at, 128)] = patch.astype(BF16)
-            at = pl.multiple_of(x * 1536, 1536)
-            act = mm(left_one[...], p_one[:, pl.ds(at, 1536)])
+                p_one[:, at + 128 * y : at + 128 * y + 128] = patch.astype(BF16)
+            act = mm(left_one[...], p_one[:, at : at + 1536])
             act = act[0:16] + act[16:32]
             gate = sigmoid(act)
             d_one[x] = gate * (1.0 + act * (1.0 - gate))
@@ -136,9 +151,6 @@
                 moved = lane_shift(cell, by) if by else cell
                 high, low = split2(moved)
                 s_two[px, py, 32 * c : 32 * c + 32, :] = jnp.concatenate([high, low], axis=0)
-        return carry
-
-    lax.fori_loop(0, 6, first, 0)
 
     ones_rows = (iota((16, 128), 0) == 0).astype(F32).astype(BF16)
     cells = []
@@ -162,12 +174,17 @@
     row, col = iota((512, 128), 0), iota((512, 128), 1)
     pick = ((row >> 7) == (col >> 5)) & ((row & 127) == 4 * (col & 31))
     parts = mm(jnp.concatenate(split3(quad), axis=0), pick.astype(F32).astype(BF16))
-    map_out[...] = xor_rows(parts[0:32] + parts[32:64] + parts[64:96], place[0], 2)
-
+    parts = parts[0:32] + parts[32:64] + parts[64:96]
+    map_out[...] = swap_last(xor_rows(parts, place[0], 2))
+
+
+def backward(
+    place, edge, p_one, d_one, p_two, d_two, left_back, up, sums, y_back, g_one
+):
     row, col = iota((128, 512), 0), iota((128, 512), 1)
     pick = ((row >> 5) == (col >> 7)) & ((row & 31) == ((col & 127) >> 2)) & ((col & 1) == 0)
-    parts = mm(jnp.concatenate(split3(up[...]), axis=0), pick.astype(F32).astype(BF16))
-    wide = (parts[0:32] + parts[32:64] + parts[64:96]) * (0.125 * scale_up)
+    parts = mm(jnp.concatenate(split3(xor_rows(swap_last(up[...]), place[0], 2)), axis=0), pick.astype(F32).astype(BF16))
+    wide = (parts[0:32] + parts[32:64] + parts[64:96]) * (0.125 * edge[12])
     highs, lows = [], []
     for x in range(4):
         for y in range(4):
@@ -208,11 +225,7 @@
                     at = (x * 12 + y) * 128
                     g_one[:, at : at + 128] = jnp.concatenate([high, low], axis=0)
 
-    def last(step, total):
-        at = pl.multiple_of(step * 3072, 3072)
-        return total + mm_nt(p_one[:, pl.ds(at, 3072)], g_one[:, pl.ds(at, 3072)])
-
-    found = lax.fori_loop(0, 6, last, jnp.zeros((224, 32), F32))
+    found = mm_nt(p_one[...], g_one[...])
     found = (found[:, 0:16] + found[:, 16:32]).reshape(28, 8, 16)
     upper = jnp.concatenate([found[:, 4:8], found[:, 0:4]], axis=1)
     found = found + upper
@@ -224,8 +237,8 @@
     sums[120:128, :] = jnp.where(low_rows, strips[2], strips[3])
 
 
-def finish(place, sums, other, mine, pooled, gk1, gb1, gk2, gb2):
-    total = sums[...] + other[...]
+def finish(place, mine, other, slots, pooled, gk1, gb1, gk2, gb2):
+    total = mine[...] + other[...]
     for g in range(27):
         s, t = g // 7, g % 7
         gk2[g] = total[16 * t : 16 * t + 16, 32 * s : 32 * s + 32]
@@ -235,32 +248,72 @@
         start = 112 + 8 * (t // 2) + 4 * (t % 2)
         gk1[g] = total[start : start + 4, 16 * s : 16 * s + 16]
     gb1[...] = total[124:125, 48:64]
-    pooled[...] = xor_rows(mine[...], place[0], 2)
-
-
-def shift_pairs(count, step):
-    return [(i, i + step) for i in range(count) if 0 <= i + step < count]
-
-
-def neighbours(block, axis, dim):
-    count = lax.axis_size(axis)
-    size = block.shape[dim]
-    low = lax.slice_in_dim(block, size - HALO, size, axis=dim)
-    high = lax.slice_in_dim(block, 0, HALO, axis=dim)
-    return (
-        lax.ppermute(low, axis, shift_pairs(count, 1)),
-        lax.ppermute(high, axis, shift_pairs(count, -1)),
-    )
-
-
-def call(kernel, outs, ins, scratch=()):
+    value = xor_rows(swap_last(slots[...]), place[0], 2)
+    turned = pltpu.roll(value, 64, 1)
+    lower = iota((1, 128), 1) < 64
+    for f in range(2):
+        for k in range(8):
+            at, near, far = slice(128 * k, 128 * k + 128), 4 * k + f, 4 * k + 2 + f
+            pooled[f, 0:1, at] = jnp.where(lower, value[near : near + 1], turned[far : far + 1])
+            pooled[f, 1:2, at] = jnp.where(lower, turned[near : near + 1], value[far : far + 1])
+
+
+def neighbours(block, axis, dim, rider=None):
+    count, size = lax.axis_size(axis), block.shape[dim]
+    to_low = lax.slice_in_dim(block, 0, HALO, axis=dim)
+    to_high = lax.slice_in_dim(block, size - HALO, size, axis=dim)
+    odd = (lax.axis_index(axis) & 1) == 1
+
+    def swap(start, value):
+        pairs = [(i, i + 1) for i in range(start, count - 1, 2)]
+        return lax.ppermute(value, axis, pairs + [(j, i) for i, j in pairs])
+
+    inner = jnp.where(odd, to_low, to_high)
+    if rider is None:
+        inner, got = swap(0, inner), None
+    else:
+        rows = inner.size // 128
+        both = swap(0, jnp.concatenate([inner.reshape(rows, 128), rider], axis=0))
+        inner, got = both[:rows].reshape(inner.shape), both[rows:]
+    outer = swap(1, jnp.where(odd, to_high, to_low))
+    return jnp.where(odd, inner, outer), jnp.where(odd, outer, inner), got
+
+
+def parts_of(slots, bit):
+    shape = slots.shape[0] // (4 << bit), 2, (2 << bit), 128
+    both = slots.reshape(shape)
+    return both[:, 0], both[:, 1]
+
+
+def joined(kept, got):
+    return jnp.stack([kept, got.reshape(kept.shape)], axis=1).reshape(32, 128)
+
+
+FLIPS = (1, 2, 4, 12)
+
+
+def flip(value, axis, by):
+    return lax.ppermute(value, axis, [(i, i ^ by) for i in range(lax.axis_size(axis))])
+
+
+def regroup(slots, bit):
+    kept, sent = parts_of(slots, bit)
+    return joined(kept, flip(sent.reshape(16, 128), "gy", FLIPS[bit]))
+
+
+def swap_last(value):
+    return jnp.concatenate([value[0:16], value[24:32], value[16:24]], axis=0)
+
+
+def call(kernel, outs, ins, scratch=(), cost=10**6):
     return pl.pallas_call(
         kernel,
         out_shape=[jax.ShapeDtypeStruct(*o) for o in outs],
         in_specs=[pl.BlockSpec(memory_space=m) for m in ins],
         out_specs=[pl.BlockSpec(memory_space=pltpu.VMEM) for _ in outs],
-        scratch_shapes=list(scratch),
-        compiler_params=VMEM,
+        scratch_shapes=[pltpu.VMEM(*s) if isinstance(s, tuple) else s for s in scratch],
+        compiler_params=pltpu.CompilerParams(vmem_limit_bytes=24 * 2**20),
+        cost_estimate=pl.CostEstimate(flops=cost, bytes_accessed=cost, transcendentals=0),
     )
 
 
@@ -269,19 +322,32 @@
     nx, ny = lax.axis_size("gx"), lax.axis_size("gy")
     vm, sm = pltpu.VMEM, pltpu.SMEM
 
-    own = jnp.transpose(volume, (1, 2, 0, 3))
-    xlo, xhi = neighbours(own, "gx", 0)
-    full = jnp.concatenate([xlo, own, xhi], axis=0)
-    ylo, yhi = neighbours(full, "gy", 1)
-
-    send = jnp.transpose(cotangent.reshape(2, 2, 16, 64), (2, 0, 1, 3)).reshape(32, 128)
-    up = lax.all_to_all(send, "gy", 0, 0, tiled=True)
+    place = gy.astype(jnp.int32).reshape(1)
 
     k1 = jnp.transpose(kernel_one, (2, 3, 4, 1, 0)).reshape(27, 4, 16)
     k2 = jnp.transpose(kernel_two, (2, 3, 4, 1, 0)).reshape(27, 16, 32)
-    left_one, left_two, left_back = call(
-        prepare, [((32, 224), BF16), ((64, 880), BF16), ((432, 128), BF16)], [vm] * 4
-    )(k1, bias_one[None], k2, bias_two[None])
+    left_one, left_two, left_back, up = call(
+        prepare,
+        [((32, 224), BF16), ((64, 880), BF16), ((432, 128), BF16), ((32, 128), F32)],
+        [sm] + [pltpu.HBM] * 5,
+        [
+            ((27, 4, 16), F32),
+            ((1, 16), F32),
+            ((27, 16, 32), F32),
+            ((1, 32), F32),
+            ((2, 2, 1024), F32),
+            pltpu.SemaphoreType.DMA((5,)),
+        ],
+    )(place, *(pltpu.with_memory_space_constraint(v, pltpu.HBM) for v in (k1, bias_one[None], k2, bias_two[None], cotangent)))
+
+    own = jnp.transpose(volume, (1, 2, 0, 3))
+    xlo, xhi, _ = neighbours(own, "gx", 0)
+    up = regroup(up, 3)
+    full = jnp.concatenate([xlo, own, xhi], axis=0)
+    kept, sent = parts_of(up, 0)
+    ylo, yhi, got = neighbours(full, "gy", 1, sent.reshape(16, 128))
+    ready = regroup(joined(kept, got), 2)
+    up = regroup(ready, 1)
 
     inside = lambda at, size, n: jnp.where(
         ((at == 0) & (jnp.arange(6) == 0)) | ((at == n - 1) & (jnp.arange(6) == 5)), 0.0, 1.0
@@ -290,43 +356,43 @@
     edge = jnp.concatenate(
         [inside(gx, 6, nx), inside(gy, 6, ny), jnp.full((4,), scale)]
     ).astype(F32)
-    place = gy.astype(jnp.int32).reshape(1)
-
-    mapped, sums = call(
-        work,
-        [((32, 128), F32), ((128, 128), F32)],
-        [sm, sm] + [vm] * 9,
+
+    p_one, d_one, p_two, d_two, mapped = call(
+        forward,
         [
-            pltpu.VMEM((14, 14, 24, 128), F32),
-            pltpu.VMEM((224, 18432), BF16),
-            pltpu.VMEM((12, 16, 1536), F32),
-            pltpu.VMEM((6, 6, 96, 128), BF16),
-            pltpu.VMEM((880, 2048), BF16),
-            pltpu.VMEM((4, 32, 512), F32),
-            pltpu.VMEM((432, 2048), F32),
-            pltpu.VMEM((32, 18432), BF16),
+            ((224, 18432), BF16),
+            ((12, 16, 1536), F32),
+            ((880, 2048), BF16),
+            ((4, 32, 512), F32),
+            ((32, 128), F32),
         ],
-    )(place, edge, xlo, own, xhi, ylo, yhi, left_one, left_two, left_back, up)
-
-    slots = mapped.reshape(2, 2, 2, 2, 2, 128)
+        [sm, sm] + [vm] * 7 + [pl.ANY],
+        [((14, 14, 24, 128), F32), ((6, 6, 96, 128), BF16)],
+        cost=10**7,
+    )(place, edge, xlo, own, xhi, ylo, yhi, left_one, left_two, ready)
+    (sums,) = call(
+        backward,
+        [((128, 128), F32)],
+        [sm, sm] + [vm] * 6,
+        [((432, 2048), F32), ((32, 18432), BF16)],
+        cost=10**7,
+    )(place, edge, p_one, d_one, p_two, d_two, left_back, up)
+
+    slots = mapped
     for bit in range(4):
-        dim = 3 - bit
-        kept, sent = (lax.index_in_dim(slots, k, dim, keepdims=True) for k in range(2))
-        packed = jnp.concatenate([sums, sent.reshape(16, 128)], axis=0)
-        got = lax.ppermute(packed, "gy", [(i, i ^ (1 << bit)) for i in range(16)])
+        kept, sent = parts_of(slots, bit)
+        got = flip(jnp.concatenate([sums, sent.reshape(16, 128)], axis=0), "gy", FLIPS[bit])
         sums = sums + got[0:128]
-        slots = jnp.concatenate([kept, got[128:144].reshape(sent.shape)], axis=dim)
-    for bit in range(3):
-        got = lax.ppermute(sums, "gx", [(i, i ^ (1 << bit)) for i in range(8)])
-        if bit < 2:
-            sums = sums + got
+        slots = joined(kept, got[128:144])
+    sums = sums + flip(sums, "gx", 4)
+    sums = sums + flip(sums, "gx", 1)
+    other = flip(sums, "gx", 3)
 
     pooled, gk1, gb1, gk2, gb2 = call(
         finish,
-        [((32, 128), F32), ((27, 4, 16), F32), ((1, 16), F32), ((27, 16, 32), F32), ((1, 32), F32)],
+        [((2, 2, 1024), F32), ((27, 4, 16), F32), ((1, 16), F32), ((27, 16, 32), F32), ((1, 32), F32)],
         [sm] + [vm] * 3,
-    )(place, sums, got, slots.reshape(32, 128))
-    pooled = jnp.transpose(pooled.reshape(16, 2, 2, 64), (1, 2, 0, 3)).reshape(2, 2, 1024)
+    )(place, sums, other, slots)
     gk1 = jnp.transpose(gk1.reshape(3, 3, 3, 4, 16), (4, 3, 0, 1, 2))
     gk2 = jnp.transpose(gk2.reshape(3, 3, 3, 16, 32), (4, 3, 0, 1, 2))
     return (pooled, gk1, gb1[0], gk2, gb2[0])

time: 87.4 us -> 67.8 us (0.78)
  the two profiles are of different devices: /device:TPU:38 before, /device:TPU:0 now
where the time goes in v2:
time: 67.8 us; the launch traced here: 67.6 us
  waiting for transfers between devices  29.5 us (44%)
  starting transfers between devices  24.5 us (36%)
  Pallas kernels  11.3 us (17%)
  local copies, waits for them, and re-layouts  1.1 us (2%)
  between operations  0.91 us (1%)
    ppermute x10, waiting for transfers between devices, flip(): lax.ppermute(value, axis, [(i, i ^ by) for i in range(lax.axis_size(axis))])  29 us
    ppermute x10, starting transfers between devices, flip(): lax.ppermute(value, axis, [(i, i ^ by) for i in range(lax.axis_size(axis))])  18.5 us
    ppermute x4, starting transfers between devices, swap(): return lax.ppermute(value, axis, pairs + [(j, i) for i, j in pairs])  5.97 us
    pallas_call x1, Pallas kernels, on_device(): call(backward, [((128, 128), F32)], [sm, sm] + [vm] * 6, [((432, 2048), F...  5.29 us
    pallas_call x1, Pallas kernels, on_device(): call(forward, [((224, 18432), BF16), ((12, 16, 1536), F32), ((880, 2048),...  3.82 us
    pallas_call x1, Pallas kernels, on_device(): call(prepare, [((32, 224), BF16), ((64, 880), BF16), ((432, 128), BF16),...  1.37 us
  transfers between devices with their start and end apart: 14, of which 10 were waited for; matrix products, arithmetic and copies ran while one was open for 0% of the time, Pallas kernels for 8%

profile of v2, /device:TPU:0, one launch (start us, length us, event | category | flops | bytes accessed | tf_op | source)
XLA Modules:
  0.0 67.6 jit_solution(13280358106496001330)
XLA Ops:
  0.6 1.0 %copy.37 = f32[4,8,8,128]{3,0,2,1:T(4,128)S(1)} copy(f32[4,8,8,128]{3,2,1,0:T(8,128)} %param.6) | data formatting | bytes 262144 | tf_op args[0]
  2.3 4.6 %collective-permute-start = (f32[3,8,4,128]{3,2,1,0:T(4,128)S(1)}, f32[3,8,4,128]{3,2,1,0:T(4,128)S(1)}, u32[]{:S(2)}, u32[]{:S(2)}) collective-permute-start(f32[3,8,4,128]{3,2,1,0:T(4,128)S(1)} %get-tuple-element.38), channel_id=1, source_target_pairs={{0,16},{32,48},{64,80},{96,112},{16,0},{48,32},{80,64},{112,96},{1... | collective-permute-start | bytes 147464 | tf_op jit(solution)/shard_map/ppermute | solution.py:269
  6.9 1.4 %shard_map.101 = (bf16[32,224]{1,0:T(8,128)(2,1)S(1)}, bf16[64,880]{1,0:T(8,128)(2,1)S(1)}, bf16[432,128]{1,0:T(8,128)(2,1)S(1)}, f32[32,128]{1,0:T(8,128)S(1)}) custom-call(s32[1]{0:T(128)} %bitcast.place, f32[27,4,16]{2,1,0:T(4,128)} %bitcast.86, f32[1,16]{1,0:T(1,128)} %bitcast.99, f32[27,16,32]{2,1,0:T(8,128)} %bitcast.81, f32[1,32]{1,0:T(1,128)} %bitcast.100, ...), custom_call_target="tpu_custom_call" | custom-call | flops 1000000 | bytes 1000000 | tf_op jit(solution)/shard_map/pallas_call | solution.py:329
  8.3 2.8 %collective-permute-start.2 = (f32[16,128]{1,0:T(8,128)S(1)}, f32[16,128]{1,0:T(8,128)S(1)}, u32[]{:S(2)}, u32[]{:S(2)}) collective-permute-start(f32[16,128]{1,0:T(8,128)S(1)} %get-tuple-element.56), channel_id=1, source_target_pairs={{0,12},{1,13},{2,14},{3,15},{4,8},{5,9},{6,10},{7,11},{8,4},{9,5},... | collective-permute-start | bytes 24584 | tf_op jit(solution)/shard_map/ppermute | solution.py:296
  11.1 2.1 %collective-permute-done.2 = f32[16,128]{1,0:T(8,128)S(1)} collective-permute-done((f32[16,128]{1,0:T(8,128)S(1)}, f32[16,128]{1,0:T(8,128)S(1)}, u32[]{:S(2)}, u32[]{:S(2)}) %collective-permute-start.2) | collective-permute-done | bytes 8224 | tf_op jit(solution)/shard_map/ppermute | solution.py:296
  14.7 6.2 %collective-permute-start.5 = (f32[16,128]{1,0:T(8,128)S(1)}, f32[16,128]{1,0:T(8,128)S(1)}, u32[]{:S(2)}, u32[]{:S(2)}) collective-permute-start(f32[16,128]{1,0:T(8,128)S(1)} %get-tuple-element.52), channel_id=1, source_target_pairs={{0,4},{1,5},{2,6},{3,7},{4,0},{5,1},{6,2},{7,3},{8,12},{9,13},{10,... | collective-permute-start | bytes 24584 | tf_op jit(solution)/shard_map/ppermute | solution.py:296
  21.1 2.3 %collective-permute-done.5 = f32[16,128]{1,0:T(8,128)S(1)} collective-permute-done((f32[16,128]{1,0:T(8,128)S(1)}, f32[16,128]{1,0:T(8,128)S(1)}, u32[]{:S(2)}, u32[]{:S(2)}) %collective-permute-start.5) | collective-permute-done | bytes 8224 | tf_op jit(solution)/shard_map/ppermute | solution.py:296
  23.4 1.4 %collective-permute-start.6 = (f32[16,128]{1,0:T(8,128)S(1)}, f32[16,128]{1,0:T(8,128)S(1)}, u32[]{:S(2)}, u32[]{:S(2)}) collective-permute-start(f32[16,128]{1,0:T(8,128)S(1)} %bitcast.97), channel_id=1, source_target_pairs={{0,2},{1,3},{2,0},{3,1},{4,6},{5,7},{6,4},{7,5},{8,10},{9,11},{10,... | collective-permute-start | bytes 24584 | tf_op jit(solution)/shard_map/ppermute | solution.py:296
  24.9 3.8 %shard_map.102 = (bf16[224,18432]{1,0:T(8,128)(2,1)S(1)}, f32[12,16,1536]{2,1,0:T(8,128)S(1)}, bf16[880,2048]{1,0:T(8,128)(2,1)S(1)}, f32[4,32,512]{2,1,0:T(8,128)S(1)}, f32[32,128]{1,0:T(8,128)S(1)}) custom-call(s32[1]{0:T(128)} %bitcast.place, f32[16]{0:T(128)S(1)} %pad_maximum_fusion.15.edge, f32[3,8,4,128]{3,2,1,0:T(4,128)S(1)} %bitcast.72, ...), custom_call_target="tpu_custom_call" | custom-call | flops 10000000 | bytes 10000000 | tf_op jit(solution)/shard_map/pallas_call | solution.py:360
  28.7 5.3 %shard_map.103 = f32[128,128]{1,0:T(8,128)S(1)} custom-call(s32[1]{0:T(128)} %bitcast.place, f32[16]{0:T(128)S(1)} %pad_maximum_fusion.15.edge, bf16[224,18432]{1,0:T(8,128)(2,1)S(1)} %get-tuple-element.22.p_one, f32[12,16,1536]{2,1,0:T(8,128)S(1)} %get-tuple-element.23.d_one, bf16[880,2048]{1,0:T(8,128)(2,1)S(1)} %get-tuple-element.24.p_two, ...), custom_call_target="tpu_custom_call" | custom-call | flops 10000000 | bytes 10000000 | tf_op jit(solution)/shard_map/pallas_call | solution.py:373
  34.0 1.2 %collective-permute-start.7 = (f32[144,128]{1,0:T(8,128)S(1)}, f32[144,128]{1,0:T(8,128)S(1)}, u32[]{:S(2)}, u32[]{:S(2)}) collective-permute-start(f32[144,128]{1,0:T(8,128)S(1)} %pad_maximum_fusion.4), channel_id=1, source_target_pairs={{0,1},{1,0},{2,3},{3,2},{4,5},{5,4},{6,7},{7,6},{8,9},{9,8},{10,11... | collective-permute-start | bytes 221192 | tf_op jit(solution)/shard_map/ppermute | solution.py:296
  35.2 0.9 %collective-permute-done.7 = f32[144,128]{1,0:T(8,128)S(1)} collective-permute-done((f32[144,128]{1,0:T(8,128)S(1)}, f32[144,128]{1,0:T(8,128)S(1)}, u32[]{:S(2)}, u32[]{:S(2)}) %collective-permute-start.7) | collective-permute-done | bytes 73760 | tf_op jit(solution)/shard_map/ppermute | solution.py:296
  36.2 1.4 %collective-permute-start.8 = (f32[144,128]{1,0:T(8,128)S(1)}, f32[144,128]{1,0:T(8,128)S(1)}, u32[]{:S(2)}, u32[]{:S(2)}) collective-permute-start(f32[144,128]{1,0:T(8,128)S(1)} %pad_maximum_fusion.5), channel_id=1, source_target_pairs={{0,2},{1,3},{2,0},{3,1},{4,6},{5,7},{6,4},{7,5},{8,10},{9,11},{10,... | collective-permute-start | bytes 221192 | tf_op jit(solution)/shard_map/ppermute | solution.py:296
  37.6 4.7 %collective-permute-done.8 = f32[144,128]{1,0:T(8,128)S(1)} collective-permute-done((f32[144,128]{1,0:T(8,128)S(1)}, f32[144,128]{1,0:T(8,128)S(1)}, u32[]{:S(2)}, u32[]{:S(2)}) %collective-permute-start.8) | collective-permute-done | bytes 73760 | tf_op jit(solution)/shard_map/ppermute | solution.py:296
  42.8 4.1 %collective-permute-done.9 = f32[144,128]{1,0:T(8,128)S(1)} collective-permute-done((f32[144,128]{1,0:T(8,128)S(1)}, f32[144,128]{1,0:T(8,128)S(1)}, u32[]{:S(2)}, u32[]{:S(2)}) %collective-permute-start.9) | collective-permute-done | bytes 73760 | tf_op jit(solution)/shard_map/ppermute | solution.py:296
  46.9 1.9 %collective-permute-start.10 = (f32[144,128]{1,0:T(8,128)S(1)}, f32[144,128]{1,0:T(8,128)S(1)}, u32[]{:S(2)}, u32[]{:S(2)}) collective-permute-start(f32[144,128]{1,0:T(8,128)S(1)} %pad_maximum_fusion.7), channel_id=1, source_target_pairs={{0,12},{1,13},{2,14},{3,15},{4,8},{5,9},{6,10},{7,11},{8,4},{9,5},... | collective-permute-start | bytes 221192 | tf_op jit(solution)/shard_map/ppermute | solution.py:296
  48.8 3.7 %collective-permute-done.10 = f32[144,128]{1,0:T(8,128)S(1)} collective-permute-done((f32[144,128]{1,0:T(8,128)S(1)}, f32[144,128]{1,0:T(8,128)S(1)}, u32[]{:S(2)}, u32[]{:S(2)}) %collective-permute-start.10) | collective-permute-done | bytes 73760 | tf_op jit(solution)/shard_map/ppermute | solution.py:296
  52.6 1.1 %collective-permute-start.11 = (f32[128,128]{1,0:T(8,128)S(1)}, f32[128,128]{1,0:T(8,128)S(1)}, u32[]{:S(2)}, u32[]{:S(2)}) collective-permute-start(f32[128,128]{1,0:T(8,128)S(1)} %slice_add_fusion), channel_id=1, source_target_pairs={{0,64},{16,80},{32,96},{48,112},{64,0},{80,16},{96,32},{112,48},{1... | collective-permute-start | bytes 196616 | tf_op jit(solution)/shard_map/ppermute | solution.py:296
  53.7 3.3 %collective-permute-done.11 = f32[128,128]{1,0:T(8,128)S(1)} collective-permute-done((f32[128,128]{1,0:T(8,128)S(1)}, f32[128,128]{1,0:T(8,128)S(1)}, u32[]{:S(2)}, u32[]{:S(2)}) %collective-permute-start.11) | collective-permute-done | bytes 65568 | tf_op jit(solution)/shard_map/ppermute | solution.py:296
  56.9 0.8 %collective-permute-start.12 = (f32[128,128]{1,0:T(8,128)S(1)}, f32[128,128]{1,0:T(8,128)S(1)}, u32[]{:S(2)}, u32[]{:S(2)}) collective-permute-start(f32[128,128]{1,0:T(8,128)S(1)} %add.22), channel_id=1, source_target_pairs={{0,16},{16,0},{32,48},{48,32},{64,80},{80,64},{96,112},{112,96},{1... | collective-permute-start | bytes 196616 | tf_op jit(solution)/shard_map/ppermute | solution.py:296
  57.7 3.5 %collective-permute-done.12 = f32[128,128]{1,0:T(8,128)S(1)} collective-permute-done((f32[128,128]{1,0:T(8,128)S(1)}, f32[128,128]{1,0:T(8,128)S(1)}, u32[]{:S(2)}, u32[]{:S(2)}) %collective-permute-start.12) | collective-permute-done | bytes 65568 | tf_op jit(solution)/shard_map/ppermute | solution.py:296
  61.3 1.2 %collective-permute-start.13 = (f32[128,128]{1,0:T(8,128)S(1)}, f32[128,128]{1,0:T(8,128)S(1)}, u32[]{:S(2)}, u32[]{:S(2)}) collective-permute-start(f32[128,128]{1,0:T(8,128)S(1)} %add.23.mine), channel_id=1, source_target_pairs={{0,48},{16,32},{32,16},{48,0},{64,112},{80,96},{96,80},{112,64},{1... | collective-permute-start | bytes 196616 | tf_op jit(solution)/shard_map/ppermute | solution.py:296
  62.5 4.3 %collective-permute-done.13.other = f32[128,128]{1,0:T(8,128)S(1)} collective-permute-done((f32[128,128]{1,0:T(8,128)S(1)}, f32[128,128]{1,0:T(8,128)S(1)}, u32[]{:S(2)}, u32[]{:S(2)}) %collective-permute-start.13) | collective-permute-done | bytes 65568 | tf_op jit(solution)/shard_map/ppermute | solution.py:296
  66.8 0.8 %shard_map.104 = (f32[2,2,1024]{2,1,0:T(2,128)}, f32[27,4,16]{2,1,0:T(4,128)}, f32[1,16]{1,0:T(1,128)}, f32[27,16,32]{2,1,0:T(8,128)}, f32[1,32]{1,0:T(1,128)}) custom-call(s32[1]{0:T(128)} %bitcast.place, f32[128,128]{1,0:T(8,128)S(1)} %add.23.mine, f32[128,128]{1,0:T(8,128)S(1)} %collective-permute-done.13.other, f32[32,128]{1,0:T(8,128)S(1)} %bitcast.76), custom_call_target="tpu_custom_call" | custom-call | flops 1000000 | bytes 1000000 | tf_op jit(solution)/shard_map/pallas_call | solution.py:391
  (54 shorter events, 2.8 us)
Async XLA Ops:
  1.7 11.6 %collective-permute-start.1 = (f32[3,8,4,128]{3,2,1,0:T(4,128)S(1)}, f32[3,8,4,128]{3,2,1,0:T(4,128)S(1)}, u32[]{:S(2)}, u32[]{:S(2)}) collective-permute-start(f32[3,8,4,128]{3,2,1,0:T(4,128)S(1)} %get-tuple-element.37), channel_id=1, source_target_pairs={{16,32},{48,64},{80,96},{32,16},{64,48},{96,80},{17,33},{49,65},{8... | collective-permute-start | bytes 147464 | tf_op jit(solution)/shard_map/ppermute | solution.py:269
  2.3 10.9 %collective-permute-start = (f32[3,8,4,128]{3,2,1,0:T(4,128)S(1)}, f32[3,8,4,128]{3,2,1,0:T(4,128)S(1)}, u32[]{:S(2)}, u32[]{:S(2)}) collective-permute-start(f32[3,8,4,128]{3,2,1,0:T(4,128)S(1)} %get-tuple-element.38), channel_id=1, source_target_pairs={{0,16},{32,48},{64,80},{96,112},{16,0},{48,32},{80,64},{112,96},{1... | collective-permute-start | bytes 147464 | tf_op jit(solution)/shard_map/ppermute | solution.py:269
  8.3 4.9 %collective-permute-start.2 = (f32[16,128]{1,0:T(8,128)S(1)}, f32[16,128]{1,0:T(8,128)S(1)}, u32[]{:S(2)}, u32[]{:S(2)}) collective-permute-start(f32[16,128]{1,0:T(8,128)S(1)} %get-tuple-element.56), channel_id=1, source_target_pairs={{0,12},{1,13},{2,14},{3,15},{4,8},{5,9},{6,10},{7,11},{8,4},{9,5},... | collective-permute-start | bytes 24584 | tf_op jit(solution)/shard_map/ppermute | solution.py:296
  13.3 1.4 %collective-permute-start.3 = (f32[184,128]{1,0:T(8,128)S(1)}, f32[184,128]{1,0:T(8,128)S(1)}, u32[]{:S(2)}, u32[]{:S(2)}) collective-permute-start(f32[184,128]{1,0:T(8,128)S(1)} %pad_maximum_fusion), channel_id=1, source_target_pairs={{0,1},{2,3},{4,5},{6,7},{8,9},{10,11},{12,13},{14,15},{1,0},{3,2},... | collective-permute-start | bytes 282632 | tf_op jit(solution)/shard_map/ppermute | solution.py:269
  13.5 7.5 %collective-permute-start.4 = (f32[14,3,4,128]{3,2,1,0:T(4,128)S(1)}, f32[14,3,4,128]{3,2,1,0:T(4,128)S(1)}, u32[]{:S(2)}, u32[]{:S(2)}) collective-permute-start(f32[14,3,4,128]{3,2,1,0:T(4,128)S(1)} %get-tuple-element.33), channel_id=1, source_target_pairs={{1,2},{3,4},{5,6},{7,8},{9,10},{11,12},{13,14},{2,1},{4,3},{6,5},{... | collective-permute-start | bytes 258056 | tf_op jit(solution)/shard_map/ppermute | solution.py:269
  14.7 8.6 %collective-permute-start.5 = (f32[16,128]{1,0:T(8,128)S(1)}, f32[16,128]{1,0:T(8,128)S(1)}, u32[]{:S(2)}, u32[]{:S(2)}) collective-permute-start(f32[16,128]{1,0:T(8,128)S(1)} %get-tuple-element.52), channel_id=1, source_target_pairs={{0,4},{1,5},{2,6},{3,7},{4,0},{5,1},{6,2},{7,3},{8,12},{9,13},{10,... | collective-permute-start | bytes 24584 | tf_op jit(solution)/shard_map/ppermute | solution.py:296
  23.4 5.3 %collective-permute-start.6 = (f32[16,128]{1,0:T(8,128)S(1)}, f32[16,128]{1,0:T(8,128)S(1)}, u32[]{:S(2)}, u32[]{:S(2)}) collective-permute-start(f32[16,128]{1,0:T(8,128)S(1)} %bitcast.97), channel_id=1, source_target_pairs={{0,2},{1,3},{2,0},{3,1},{4,6},{5,7},{6,4},{7,5},{8,10},{9,11},{10,... | collective-permute-start | bytes 24584 | tf_op jit(solution)/shard_map/ppermute | solution.py:296
  34.0 2.1 %collective-permute-start.7 = (f32[144,128]{1,0:T(8,128)S(1)}, f32[144,128]{1,0:T(8,128)S(1)}, u32[]{:S(2)}, u32[]{:S(2)}) collective-permute-start(f32[144,128]{1,0:T(8,128)S(1)} %pad_maximum_fusion.4), channel_id=1, source_target_pairs={{0,1},{1,0},{2,3},{3,2},{4,5},{5,4},{6,7},{7,6},{8,9},{9,8},{10,11... | collective-permute-start | bytes 221192 | tf_op jit(solution)/shard_map/ppermute | solution.py:296
  36.2 6.1 %collective-permute-start.8 = (f32[144,128]{1,0:T(8,128)S(1)}, f32[144,128]{1,0:T(8,128)S(1)}, u32[]{:S(2)}, u32[]{:S(2)}) collective-permute-start(f32[144,128]{1,0:T(8,128)S(1)} %pad_maximum_fusion.5), channel_id=1, source_target_pairs={{0,2},{1,3},{2,0},{3,1},{4,6},{5,7},{6,4},{7,5},{8,10},{9,11},{10,... | collective-permute-start | bytes 221192 | tf_op jit(solution)/shard_map/ppermute | solution.py:296
  42.4 4.4 %collective-permute-start.9 = (f32[144,128]{1,0:T(8,128)S(1)}, f32[144,128]{1,0:T(8,128)S(1)}, u32[]{:S(2)}, u32[]{:S(2)}) collective-permute-start(f32[144,128]{1,0:T(8,128)S(1)} %pad_maximum_fusion.6), channel_id=1, source_target_pairs={{0,4},{1,5},{2,6},{3,7},{4,0},{5,1},{6,2},{7,3},{8,12},{9,13},{10,... | collective-permute-start | bytes 221192 | tf_op jit(solution)/shard_map/ppermute | solution.py:296
  46.9 5.6 %collective-permute-start.10 = (f32[144,128]{1,0:T(8,128)S(1)}, f32[144,128]{1,0:T(8,128)S(1)}, u32[]{:S(2)}, u32[]{:S(2)}) collective-permute-start(f32[144,128]{1,0:T(8,128)S(1)} %pad_maximum_fusion.7), channel_id=1, source_target_pairs={{0,12},{1,13},{2,14},{3,15},{4,8},{5,9},{6,10},{7,11},{8,4},{9,5},... | collective-permute-start | bytes 221192 | tf_op jit(solution)/shard_map/ppermute | solution.py:296
  52.6 4.3 %collective-permute-start.11 = (f32[128,128]{1,0:T(8,128)S(1)}, f32[128,128]{1,0:T(8,128)S(1)}, u32[]{:S(2)}, u32[]{:S(2)}) collective-permute-start(f32[128,128]{1,0:T(8,128)S(1)} %slice_add_fusion), channel_id=1, source_target_pairs={{0,64},{16,80},{32,96},{48,112},{64,0},{80,16},{96,32},{112,48},{1... | collective-permute-start | bytes 196616 | tf_op jit(solution)/shard_map/ppermute | solution.py:296
  56.9 4.3 %collective-permute-start.12 = (f32[128,128]{1,0:T(8,128)S(1)}, f32[128,128]{1,0:T(8,128)S(1)}, u32[]{:S(2)}, u32[]{:S(2)}) collective-permute-start(f32[128,128]{1,0:T(8,128)S(1)} %add.22), channel_id=1, source_target_pairs={{0,16},{16,0},{32,48},{48,32},{64,80},{80,64},{96,112},{112,96},{1... | collective-permute-start | bytes 196616 | tf_op jit(solution)/shard_map/ppermute | solution.py:296
  61.3 5.6 %collective-permute-start.13 = (f32[128,128]{1,0:T(8,128)S(1)}, f32[128,128]{1,0:T(8,128)S(1)}, u32[]{:S(2)}, u32[]{:S(2)}) collective-permute-start(f32[128,128]{1,0:T(8,128)S(1)} %add.23.mine), channel_id=1, source_target_pairs={{0,48},{16,32},{32,16},{48,0},{64,112},{80,96},{96,80},{112,64},{1... | collective-permute-start | bytes 196616 | tf_op jit(solution)/shard_map/ppermute | solution.py:296

commit v3 on v2

--- a/solution.py
+++ b/solution.py
@@ -10,6 +10,7 @@
 F32, BF16 = jnp.float32, jnp.bfloat16
 HALO = 3
 TAPS = [(a, b) for a in range(3) for b in range(3)]
+TAPS_ONE = [(a, b) for b in range(3) for a in range(3)]
 NT = (((1,), (1,)), ((), ()))
 
 
@@ -95,7 +96,8 @@
             rows[4 * k + 2 + f] = jnp.where(lower, pltpu.roll(near, 64, 1), far)
     send[...] = swap_last(xor_rows(jnp.concatenate(rows, axis=0), place[0], 2))
 
-    taps = [jnp.concatenate([k1[t], k1[t]], axis=0) for t in range(27)]
+    order = [(a * 3 + b) * 3 + c for a, b in TAPS_ONE for c in range(3)]
+    taps = [jnp.concatenate([k1[t], k1[t]], axis=0) for t in order]
     whole = jnp.concatenate(taps + [ones_first(b1[...], 8)], axis=0)
     high, low = split2(whole)
     left_one[0:16, :] = mm_nt(eye(16), high).astype(BF16)
@@ -116,10 +118,8 @@
     return jnp.concatenate([lane_shift(both, 1), both, lane_shift(both, -1)], axis=1)
 
 
-def forward(
-    place, edge, xlo, own, xhi, ylo, yhi, left_one, left_two, unused,
-    p_one, d_one, p_two, d_two, map_out,
-    s_one, s_two,
+def forward_one(
+    edge, xlo, own, xhi, ylo, yhi, left_one, unused, p_one, d_one, s_two, s_one
 ):
     for ref, start in ((xlo, 0), (own, HALO), (xhi, HALO + own.shape[0])):
         for x in range(ref.shape[0]):
@@ -135,7 +135,7 @@
         for x in (2 * px, 2 * px + 1):
             at = 1536 * x
             for y in range(12):
-                patch = jnp.concatenate([s_one[x + a, y + b] for a, b in TAPS] + [one_row], axis=0)
+                patch = jnp.concatenate([s_one[x + a, y + b] for a, b in TAPS_ONE] + [one_row], axis=0)
                 p_one[:, at + 128 * y : at + 128 * y + 128] = patch.astype(BF16)
             act = mm(left_one[...], p_one[:, at : at + 1536])
             act = act[0:16] + act[16:32]
@@ -152,6 +152,8 @@
                 high, low = split2(moved)
                 s_two[px, py, 32 * c : 32 * c + 32, :] = jnp.concatenate([high, low], axis=0)
 
+
+def forward_two(place, s_two, left_two, unused, p_two, d_two, map_out):
     ones_rows = (iota((16, 128), 0) == 0).astype(F32).astype(BF16)
     cells = []
     for x in range(4):
@@ -204,7 +206,14 @@
     slots = [jnp.concatenate(groups[7 * s : 7 * s + 7], axis=0)[:, 0:32] for s in range(4)]
     sums[0:112, :] = jnp.concatenate(slots, axis=1)
 
+    blank = jnp.zeros((32, 128), F32).astype(BF16)
+    whole = jnp.zeros((16, 128), F32)
+    found = jnp.zeros((80, 96), F32)
     for px in range(6):
+        for x in (2 * px, 2 * px + 1):
+            for b, y in ((0, 12), (0, 13), (1, 0), (1, 13), (2, 0), (2, 1)):
+                at = (x * 14 + y) * 128
+                g_one[32 * b : 32 * b + 32, at : at + 128] = blank
         for py in range(6):
             acc = [None] * 3
             for a, b in TAPS:
@@ -221,14 +230,23 @@
             for dx in range(2):
                 for dy in range(2):
                     x, y = 2 * px + dx, 2 * py + dy
-                    high, low = split2(cell * d_one[x, :, 128 * y : 128 * y + 128])
-                    at = (x * 12 + y) * 128
-                    g_one[:, at : at + 128] = jnp.concatenate([high, low], axis=0)
-
-    found = mm_nt(p_one[...], g_one[...])
-    found = (found[:, 0:16] + found[:, 16:32]).reshape(28, 8, 16)
-    upper = jnp.concatenate([found[:, 4:8], found[:, 0:4]], axis=1)
-    found = found + upper
+                    grad = cell * d_one[x, :, 128 * y : 128 * y + 128]
+                    whole = whole + grad
+                    both = jnp.concatenate(split2(grad), axis=0)
+                    for b in range(3):
+                        at = (x * 14 + y + b) * 128
+                        g_one[32 * b : 32 * b + 32, at : at + 128] = both
+        for x in (2 * px, 2 * px + 1):
+            at, to = 1536 * x, 1792 * x
+            found = found + mm_nt(p_one[0:80, at : at + 1536], g_one[:, to : to + 1536])
+            found = found + mm_nt(p_one[144:224, at + 1280 : at + 1536], g_one[:, to + 1536 : to + 1792])
+
+    by_b = [found[:, 32 * b : 32 * b + 16] + found[:, 32 * b + 16 : 32 * b + 32] for b in range(3)]
+    groups = [by_b[b][(a * 3 + c) * 8 : (a * 3 + c) * 8 + 8] for a, b in TAPS for c in range(3)]
+    ones = (iota((8, 128), 0) == 0).astype(F32).astype(BF16)
+    groups.append(sum(mm_nt(ones, part) for part in split3(whole)))
+    found = jnp.concatenate(groups, axis=0).reshape(28, 8, 16)
+    found = found + jnp.concatenate([found[:, 4:8], found[:, 0:4]], axis=1)
     blank = jnp.zeros((8, 16), F32)
     blocks = [found[g] for g in range(28)] + [blank] * 4
     strips = [jnp.concatenate(blocks[8 * t : 8 * t + 8], axis=1) for t in range(4)]
@@ -258,7 +276,7 @@
             pooled[f, 1:2, at] = jnp.where(lower, turned[near : near + 1], value[far : far + 1])
 
 
-def neighbours(block, axis, dim, rider=None):
+def neighbours(block, axis, dim):
     count, size = lax.axis_size(axis), block.shape[dim]
     to_low = lax.slice_in_dim(block, 0, HALO, axis=dim)
     to_high = lax.slice_in_dim(block, size - HALO, size, axis=dim)
@@ -268,15 +286,9 @@
         pairs = [(i, i + 1) for i in range(start, count - 1, 2)]
         return lax.ppermute(value, axis, pairs + [(j, i) for i, j in pairs])
 
-    inner = jnp.where(odd, to_low, to_high)
-    if rider is None:
-        inner, got = swap(0, inner), None
-    else:
-        rows = inner.size // 128
-        both = swap(0, jnp.concatenate([inner.reshape(rows, 128), rider], axis=0))
-        inner, got = both[:rows].reshape(inner.shape), both[rows:]
+    inner = swap(0, jnp.where(odd, to_low, to_high))
     outer = swap(1, jnp.where(odd, to_high, to_low))
-    return jnp.where(odd, inner, outer), jnp.where(odd, outer, inner), got
+    return jnp.where(odd, inner, outer), jnp.where(odd, outer, inner), inner
 
 
 def parts_of(slots, bit):
@@ -299,6 +311,10 @@
 def regroup(slots, bit):
     kept, sent = parts_of(slots, bit)
     return joined(kept, flip(sent.reshape(16, 128), "gy", FLIPS[bit]))
+
+
+def after(rows, other):
+    return rows + 0.0 * other[(0,) * (other.ndim - 1)][None]
 
 
 def swap_last(value):
@@ -342,12 +358,12 @@
 
     own = jnp.transpose(volume, (1, 2, 0, 3))
     xlo, xhi, _ = neighbours(own, "gx", 0)
-    up = regroup(up, 3)
     full = jnp.concatenate([xlo, own, xhi], axis=0)
-    kept, sent = parts_of(up, 0)
-    ylo, yhi, got = neighbours(full, "gy", 1, sent.reshape(16, 128))
-    ready = regroup(joined(kept, got), 2)
-    up = regroup(ready, 1)
+    ylo, yhi, inner = neighbours(full, "gy", 1)
+    turn_one = regroup(up, 3)
+    turn_two = regroup(after(turn_one, inner), 2)
+    turn_three = regroup(turn_two, 1)
+    up = regroup(turn_three, 0)
 
     inside = lambda at, size, n: jnp.where(
         ((at == 0) & (jnp.arange(6) == 0)) | ((at == n - 1) & (jnp.arange(6) == 5)), 0.0, 1.0
@@ -357,24 +373,24 @@
         [inside(gx, 6, nx), inside(gy, 6, ny), jnp.full((4,), scale)]
     ).astype(F32)
 
-    p_one, d_one, p_two, d_two, mapped = call(
-        forward,
-        [
-            ((224, 18432), BF16),
-            ((12, 16, 1536), F32),
-            ((880, 2048), BF16),
-            ((4, 32, 512), F32),
-            ((32, 128), F32),
-        ],
-        [sm, sm] + [vm] * 7 + [pl.ANY],
-        [((14, 14, 24, 128), F32), ((6, 6, 96, 128), BF16)],
+    p_one, d_one, s_two = call(
+        forward_one,
+        [((224, 18432), BF16), ((12, 16, 1536), F32), ((6, 6, 96, 128), BF16)],
+        [sm] + [vm] * 6 + [pl.ANY],
+        [((14, 14, 24, 128), F32)],
         cost=10**7,
-    )(place, edge, xlo, own, xhi, ylo, yhi, left_one, left_two, ready)
+    )(edge, xlo, own, xhi, ylo, yhi, left_one, turn_two)
+    p_two, d_two, mapped = call(
+        forward_two,
+        [((880, 2048), BF16), ((4, 32, 512), F32), ((32, 128), F32)],
+        [sm] + [vm] * 2 + [pl.ANY],
+        cost=10**7,
+    )(place, s_two, left_two, turn_three)
     (sums,) = call(
         backward,
         [((128, 128), F32)],
         [sm, sm] + [vm] * 6,
-        [((432, 2048), F32), ((32, 18432), BF16)],
+        [((432, 2048), F32), ((96, 21504), BF16)],
         cost=10**7,
     )(place, edge, p_one, d_one, p_two, d_two, left_back, up)
 

time: 67.8 us -> 64.1 us (0.945)
  waiting for transfers between devices: 29.5 us -> 24.7 us
  starting transfers between devices: 24.5 us -> 26.5 us
  Pallas kernels: 11.3 us -> 10.4 us
    ppermute x10 -> x11, waiting for transfers between devices: 29 us -> 23.4 us  [flip(): lax.ppermute(value, axis, [(i, i ^ by) for i in range(lax.axis_size(axis))])]
    ppermute x10 -> x11, starting transfers between devices: 18.5 us -> 20.5 us  [flip(): lax.ppermute(value, axis, [(i, i ^ by) for i in range(lax.axis_size(axis))])]
    pallas_call x1, Pallas kernels: 5.29 us -> 3.95 us  [on_device(): call(backward, [((128, 128), F32)], [sm, sm] + [vm] * 6, [((432, 2048), F...]
    ppermute x4, waiting for transfers between devices: 0.54 us -> 1.26 us  [swap(): return lax.ppermute(value, axis, pairs + [(j, i) for i, j in pairs])]
    pallas_call x1 -> x2, Pallas kernels: 3.82 us -> 4.28 us  [the longest x1 3.03 us: on_device(): call(forward_one, [((224, 18432), BF16), ((12, 16, 1536), F32), ((6, 6, 9...]
  transfers between devices with their start and end apart: 14 -> 15, of which waited for: 10 -> 10; matrix products, arithmetic and copies ran while one was open for 0% -> 0% of each run, Pallas kernels for 8% -> 9%
where the time goes in v3:
time: 64.1 us; the launch traced here: 63.9 us
  starting transfers between devices  26.5 us (41%)
  waiting for transfers between devices  24.7 us (39%)
  Pallas kernels  10.4 us (16%)
  local copies, waits for them, and re-layouts  1.09 us (2%)
  between operations  0.9 us (1%)
    ppermute x11, waiting for transfers between devices, flip(): lax.ppermute(value, axis, [(i, i ^ by) for i in range(lax.axis_size(axis))])  23.4 us
    ppermute x11, starting transfers between devices, flip(): lax.ppermute(value, axis, [(i, i ^ by) for i in range(lax.axis_size(axis))])  20.5 us
    ppermute x4, starting transfers between devices, swap(): return lax.ppermute(value, axis, pairs + [(j, i) for i, j in pairs])  5.96 us
    pallas_call x1, Pallas kernels, on_device(): call(backward, [((128, 128), F32)], [sm, sm] + [vm] * 6, [((432, 2048), F...  3.95 us
    pallas_call x1, Pallas kernels, on_device(): call(forward_one, [((224, 18432), BF16), ((12, 16, 1536), F32), ((6, 6, 9...  3.03 us
    pallas_call x1, Pallas kernels, on_device(): call(prepare, [((32, 224), BF16), ((64, 880), BF16), ((432, 128), BF16),...  1.37 us
  transfers between devices with their start and end apart: 15, of which 10 were waited for; matrix products, arithmetic and copies ran while one was open for 0% of the time, Pallas kernels for 9%

profile of v3, /device:TPU:0, one launch (start us, length us, event | category | flops | bytes accessed | tf_op | source)
XLA Modules:
  0.0 63.9 jit_solution(4902050075814101696)
XLA Ops:
  0.6 1.0 %copy.34 = f32[4,8,8,128]{3,0,2,1:T(4,128)S(1)} copy(f32[4,8,8,128]{3,2,1,0:T(8,128)} %param.6) | data formatting | bytes 262144 | tf_op args[0]
  2.3 4.6 %collective-permute-start = (f32[3,8,4,128]{3,2,1,0:T(4,128)S(1)}, f32[3,8,4,128]{3,2,1,0:T(4,128)S(1)}, u32[]{:S(2)}, u32[]{:S(2)}) collective-permute-start(f32[3,8,4,128]{3,2,1,0:T(4,128)S(1)} %get-tuple-element.40), channel_id=1, source_target_pairs={{0,16},{32,48},{64,80},{96,112},{16,0},{48,32},{80,64},{112,96},{1... | collective-permute-start | bytes 147464 | tf_op jit(solution)/shard_map/ppermute | solution.py:287
  6.9 1.4 %shard_map.101 = (bf16[32,224]{1,0:T(8,128)(2,1)S(1)}, bf16[64,880]{1,0:T(8,128)(2,1)S(1)}, bf16[432,128]{1,0:T(8,128)(2,1)S(1)}, f32[32,128]{1,0:T(8,128)S(1)}) custom-call(s32[1]{0:T(128)} %bitcast.place, f32[27,4,16]{2,1,0:T(4,128)} %bitcast.84, f32[1,16]{1,0:T(1,128)} %bitcast.97, f32[27,16,32]{2,1,0:T(8,128)} %bitcast.81, f32[1,32]{1,0:T(1,128)} %bitcast.98, ...), custom_call_target="tpu_custom_call" | custom-call | flops 1000000 | bytes 1000000 | tf_op jit(solution)/shard_map/pallas_call | solution.py:345
  8.3 2.8 %collective-permute-start.4 = (f32[16,128]{1,0:T(8,128)S(1)}, f32[16,128]{1,0:T(8,128)S(1)}, u32[]{:S(2)}, u32[]{:S(2)}) collective-permute-start(f32[16,128]{1,0:T(8,128)S(1)} %get-tuple-element.58), channel_id=1, source_target_pairs={{0,12},{1,13},{2,14},{3,15},{4,8},{5,9},{6,10},{7,11},{8,4},{9,5},... | collective-permute-start | bytes 24584 | tf_op jit(solution)/shard_map/ppermute | solution.py:308
  11.3 1.3 %collective-permute-done.2 = f32[14,3,4,128]{3,2,1,0:T(4,128)S(1)} collective-permute-done((f32[14,3,4,128]{3,2,1,0:T(4,128)S(1)}, f32[14,3,4,128]{3,2,1,0:T(4,128)S(1)}, u32[]{:S(2)}, u32[]{:S(2)}) %collective-permute-start.2) | collective-permute-done | bytes 86048 | tf_op jit(solution)/shard_map/ppermute | solution.py:287
  14.3 2.6 %collective-permute-done.5 = f32[16,128]{1,0:T(8,128)S(1)} collective-permute-done((f32[16,128]{1,0:T(8,128)S(1)}, f32[16,128]{1,0:T(8,128)S(1)}, u32[]{:S(2)}, u32[]{:S(2)}) %collective-permute-start.5) | collective-permute-done | bytes 8224 | tf_op jit(solution)/shard_map/ppermute | solution.py:308
  16.9 3.9 %collective-permute-start.6 = (f32[16,128]{1,0:T(8,128)S(1)}, f32[16,128]{1,0:T(8,128)S(1)}, u32[]{:S(2)}, u32[]{:S(2)}) collective-permute-start(f32[16,128]{1,0:T(8,128)S(1)} %bitcast.93), channel_id=1, source_target_pairs={{0,2},{1,3},{2,0},{3,1},{4,6},{5,7},{6,4},{7,5},{8,10},{9,11},{10,... | collective-permute-start | bytes 24584 | tf_op jit(solution)/shard_map/ppermute | solution.py:308
  20.8 3.0 %shard_map.102 = (bf16[224,18432]{1,0:T(8,128)(2,1)S(1)}, f32[12,16,1536]{2,1,0:T(8,128)S(1)}, bf16[6,6,96,128]{3,2,1,0:T(8,128)(2,1)S(1)}) custom-call(f32[16]{0:T(128)S(1)} %pad_maximum_fusion.13.edge, f32[3,8,4,128]{3,2,1,0:T(4,128)S(1)} %bitcast.72, f32[8,8,4,128]{3,2,1,0:T(4,128)S(1)} %bitcast.68, f32[3,8,4,128]{3,2,1,0:T(4,128)S(1)} %bitcast.70, ...), custom_call_target="tpu_custom_call" | custom-call | flops 10000000 | bytes 10000000 | tf_op jit(solution)/shard_map/pallas_call | solution.py:376
  23.9 1.1 %collective-permute-start.7 = (f32[16,128]{1,0:T(8,128)S(1)}, f32[16,128]{1,0:T(8,128)S(1)}, u32[]{:S(2)}, u32[]{:S(2)}) collective-permute-start(f32[16,128]{1,0:T(8,128)S(1)} %bitcast.96), channel_id=1, source_target_pairs={{0,1},{1,0},{2,3},{3,2},{4,5},{5,4},{6,7},{7,6},{8,9},{9,8},{10,11... | collective-permute-start | bytes 24584 | tf_op jit(solution)/shard_map/ppermute | solution.py:308
  25.0 1.3 %shard_map.103 = (bf16[880,2048]{1,0:T(8,128)(2,1)S(1)}, f32[4,32,512]{2,1,0:T(8,128)S(1)}, f32[32,128]{1,0:T(8,128)S(1)}) custom-call(s32[1]{0:T(128)} %bitcast.place, bf16[6,6,96,128]{3,2,1,0:T(8,128)(2,1)S(1)} %get-tuple-element.24.s_two, bf16[64,880]{1,0:T(8,128)(2,1)S(1)} %get-tuple-element.25.left_two, f32[32,128]{1,0:T(8,128)S(1)} %bitcast.74), custom_call_target="tpu_custom_call" | custom-call | flops 10000000 | bytes 10000000 | tf_op jit(solution)/shard_map/pallas_call | solution.py:383
  26.3 3.9 %shard_map.104 = f32[128,128]{1,0:T(8,128)S(1)} custom-call(s32[1]{0:T(128)} %bitcast.place, f32[16]{0:T(128)S(1)} %pad_maximum_fusion.13.edge, bf16[224,18432]{1,0:T(8,128)(2,1)S(1)} %get-tuple-element.22.p_one, f32[12,16,1536]{2,1,0:T(8,128)S(1)} %get-tuple-element.23.d_one, bf16[880,2048]{1,0:T(8,128)(2,1)S(1)} %get-tuple-element.26.p_two, ...), custom_call_target="tpu_custom_call" | custom-call | flops 10000000 | bytes 10000000 | tf_op jit(solution)/shard_map/pallas_call | solution.py:389
  30.4 1.2 %collective-permute-done.8 = f32[144,128]{1,0:T(8,128)S(1)} collective-permute-done((f32[144,128]{1,0:T(8,128)S(1)}, f32[144,128]{1,0:T(8,128)S(1)}, u32[]{:S(2)}, u32[]{:S(2)}) %collective-permute-start.8) | collective-permute-done | bytes 73760 | tf_op jit(solution)/shard_map/ppermute | solution.py:308
  31.7 4.1 %collective-permute-start.9 = (f32[144,128]{1,0:T(8,128)S(1)}, f32[144,128]{1,0:T(8,128)S(1)}, u32[]{:S(2)}, u32[]{:S(2)}) collective-permute-start(f32[144,128]{1,0:T(8,128)S(1)} %pad_maximum_fusion.4), channel_id=1, source_target_pairs={{0,2},{1,3},{2,0},{3,1},{4,6},{5,7},{6,4},{7,5},{8,10},{9,11},{10,... | collective-permute-start | bytes 221192 | tf_op jit(solution)/shard_map/ppermute | solution.py:308
  35.8 2.8 %collective-permute-done.9 = f32[144,128]{1,0:T(8,128)S(1)} collective-permute-done((f32[144,128]{1,0:T(8,128)S(1)}, f32[144,128]{1,0:T(8,128)S(1)}, u32[]{:S(2)}, u32[]{:S(2)}) %collective-permute-start.9) | collective-permute-done | bytes 73760 | tf_op jit(solution)/shard_map/ppermute | solution.py:308
  38.7 1.9 %collective-permute-start.10 = (f32[144,128]{1,0:T(8,128)S(1)}, f32[144,128]{1,0:T(8,128)S(1)}, u32[]{:S(2)}, u32[]{:S(2)}) collective-permute-start(f32[144,128]{1,0:T(8,128)S(1)} %pad_maximum_fusion.5), channel_id=1, source_target_pairs={{0,4},{1,5},{2,6},{3,7},{4,0},{5,1},{6,2},{7,3},{8,12},{9,13},{10,... | collective-permute-start | bytes 221192 | tf_op jit(solution)/shard_map/ppermute | solution.py:308
  40.6 2.5 %collective-permute-done.10 = f32[144,128]{1,0:T(8,128)S(1)} collective-permute-done((f32[144,128]{1,0:T(8,128)S(1)}, f32[144,128]{1,0:T(8,128)S(1)}, u32[]{:S(2)}, u32[]{:S(2)}) %collective-permute-start.10) | collective-permute-done | bytes 73760 | tf_op jit(solution)/shard_map/ppermute | solution.py:308
  43.2 2.3 %collective-permute-start.11 = (f32[144,128]{1,0:T(8,128)S(1)}, f32[144,128]{1,0:T(8,128)S(1)}, u32[]{:S(2)}, u32[]{:S(2)}) collective-permute-start(f32[144,128]{1,0:T(8,128)S(1)} %pad_maximum_fusion.6), channel_id=1, source_target_pairs={{0,12},{1,13},{2,14},{3,15},{4,8},{5,9},{6,10},{7,11},{8,4},{9,5},... | collective-permute-start | bytes 221192 | tf_op jit(solution)/shard_map/ppermute | solution.py:308
  45.5 3.3 %collective-permute-done.11 = f32[144,128]{1,0:T(8,128)S(1)} collective-permute-done((f32[144,128]{1,0:T(8,128)S(1)}, f32[144,128]{1,0:T(8,128)S(1)}, u32[]{:S(2)}, u32[]{:S(2)}) %collective-permute-start.11) | collective-permute-done | bytes 73760 | tf_op jit(solution)/shard_map/ppermute | solution.py:308
  48.8 1.1 %collective-permute-start.12 = (f32[128,128]{1,0:T(8,128)S(1)}, f32[128,128]{1,0:T(8,128)S(1)}, u32[]{:S(2)}, u32[]{:S(2)}) collective-permute-start(f32[128,128]{1,0:T(8,128)S(1)} %slice_add_fusion), channel_id=1, source_target_pairs={{0,64},{16,80},{32,96},{48,112},{64,0},{80,16},{96,32},{112,48},{1... | collective-permute-start | bytes 196616 | tf_op jit(solution)/shard_map/ppermute | solution.py:308
  50.0 3.2 %collective-permute-done.12 = f32[128,128]{1,0:T(8,128)S(1)} collective-permute-done((f32[128,128]{1,0:T(8,128)S(1)}, f32[128,128]{1,0:T(8,128)S(1)}, u32[]{:S(2)}, u32[]{:S(2)}) %collective-permute-start.12) | collective-permute-done | bytes 65568 | tf_op jit(solution)/shard_map/ppermute | solution.py:308
  54.0 3.5 %collective-permute-done.13 = f32[128,128]{1,0:T(8,128)S(1)} collective-permute-done((f32[128,128]{1,0:T(8,128)S(1)}, f32[128,128]{1,0:T(8,128)S(1)}, u32[]{:S(2)}, u32[]{:S(2)}) %collective-permute-start.13) | collective-permute-done | bytes 65568 | tf_op jit(solution)/shard_map/ppermute | solution.py:308
  57.5 2.0 %collective-permute-start.14 = (f32[128,128]{1,0:T(8,128)S(1)}, f32[128,128]{1,0:T(8,128)S(1)}, u32[]{:S(2)}, u32[]{:S(2)}) collective-permute-start(f32[128,128]{1,0:T(8,128)S(1)} %add.34.mine), channel_id=1, source_target_pairs={{0,48},{16,32},{32,16},{48,0},{64,112},{80,96},{96,80},{112,64},{1... | collective-permute-start | bytes 196616 | tf_op jit(solution)/shard_map/ppermute | solution.py:308
  59.6 3.5 %collective-permute-done.14.other = f32[128,128]{1,0:T(8,128)S(1)} collective-permute-done((f32[128,128]{1,0:T(8,128)S(1)}, f32[128,128]{1,0:T(8,128)S(1)}, u32[]{:S(2)}, u32[]{:S(2)}) %collective-permute-start.14) | collective-permute-done | bytes 65568 | tf_op jit(solution)/shard_map/ppermute | solution.py:308
  63.1 0.8 %shard_map.105 = (f32[2,2,1024]{2,1,0:T(2,128)}, f32[27,4,16]{2,1,0:T(4,128)}, f32[1,16]{1,0:T(1,128)}, f32[27,16,32]{2,1,0:T(8,128)}, f32[1,32]{1,0:T(1,128)}) custom-call(s32[1]{0:T(128)} %bitcast.place, f32[128,128]{1,0:T(8,128)S(1)} %add.34.mine, f32[128,128]{1,0:T(8,128)S(1)} %collective-permute-done.14.other, f32[32,128]{1,0:T(8,128)S(1)} %bitcast.78), custom_call_target="tpu_custom_call" | custom-call | flops 1000000 | bytes 1000000 | tf_op jit(solution)/shard_map/pallas_call | solution.py:407
  (55 shorter events, 3.7 us)
Async XLA Ops:
  1.7 9.5 %collective-permute-start.1 = (f32[3,8,4,128]{3,2,1,0:T(4,128)S(1)}, f32[3,8,4,128]{3,2,1,0:T(4,128)S(1)}, u32[]{:S(2)}, u32[]{:S(2)}) collective-permute-start(f32[3,8,4,128]{3,2,1,0:T(4,128)S(1)} %get-tuple-element.39), channel_id=1, source_target_pairs={{16,32},{48,64},{80,96},{32,16},{64,48},{96,80},{17,33},{49,65},{8... | collective-permute-start | bytes 147464 | tf_op jit(solution)/shard_map/ppermute | solution.py:287
  2.3 8.8 %collective-permute-start = (f32[3,8,4,128]{3,2,1,0:T(4,128)S(1)}, f32[3,8,4,128]{3,2,1,0:T(4,128)S(1)}, u32[]{:S(2)}, u32[]{:S(2)}) collective-permute-start(f32[3,8,4,128]{3,2,1,0:T(4,128)S(1)} %get-tuple-element.40), channel_id=1, source_target_pairs={{0,16},{32,48},{64,80},{96,112},{16,0},{48,32},{80,64},{112,96},{1... | collective-permute-start | bytes 147464 | tf_op jit(solution)/shard_map/ppermute | solution.py:287
  8.3 4.9 %collective-permute-start.4 = (f32[16,128]{1,0:T(8,128)S(1)}, f32[16,128]{1,0:T(8,128)S(1)}, u32[]{:S(2)}, u32[]{:S(2)}) collective-permute-start(f32[16,128]{1,0:T(8,128)S(1)} %get-tuple-element.58), channel_id=1, source_target_pairs={{0,12},{1,13},{2,14},{3,15},{4,8},{5,9},{6,10},{7,11},{8,4},{9,5},... | collective-permute-start | bytes 24584 | tf_op jit(solution)/shard_map/ppermute | solution.py:308
  11.2 1.4 %collective-permute-start.2 = (f32[14,3,4,128]{3,2,1,0:T(4,128)S(1)}, f32[14,3,4,128]{3,2,1,0:T(4,128)S(1)}, u32[]{:S(2)}, u32[]{:S(2)}) collective-permute-start(f32[14,3,4,128]{3,2,1,0:T(4,128)S(1)} %get-tuple-element.36), channel_id=1, source_target_pairs={{0,1},{2,3},{4,5},{6,7},{8,9},{10,11},{12,13},{14,15},{1,0},{3,2},... | collective-permute-start | bytes 258056 | tf_op jit(solution)/shard_map/ppermute | solution.py:287
  13.2 3.7 %collective-permute-start.5 = (f32[16,128]{1,0:T(8,128)S(1)}, f32[16,128]{1,0:T(8,128)S(1)}, u32[]{:S(2)}, u32[]{:S(2)}) collective-permute-start(f32[16,128]{1,0:T(8,128)S(1)} %get-tuple-element.56), channel_id=1, source_target_pairs={{0,4},{1,5},{2,6},{3,7},{4,0},{5,1},{6,2},{7,3},{8,12},{9,13},{10,... | collective-permute-start | bytes 24584 | tf_op jit(solution)/shard_map/ppermute | solution.py:308
  13.6 7.2 %collective-permute-start.3 = (f32[14,3,4,128]{3,2,1,0:T(4,128)S(1)}, f32[14,3,4,128]{3,2,1,0:T(4,128)S(1)}, u32[]{:S(2)}, u32[]{:S(2)}) collective-permute-start(f32[14,3,4,128]{3,2,1,0:T(4,128)S(1)} %get-tuple-element.35), channel_id=1, source_target_pairs={{1,2},{3,4},{5,6},{7,8},{9,10},{11,12},{13,14},{2,1},{4,3},{6,5},{... | collective-permute-start | bytes 258056 | tf_op jit(solution)/shard_map/ppermute | solution.py:287
  16.9 7.0 %collective-permute-start.6 = (f32[16,128]{1,0:T(8,128)S(1)}, f32[16,128]{1,0:T(8,128)S(1)}, u32[]{:S(2)}, u32[]{:S(2)}) collective-permute-start(f32[16,128]{1,0:T(8,128)S(1)} %bitcast.93), channel_id=1, source_target_pairs={{0,2},{1,3},{2,0},{3,1},{4,6},{5,7},{6,4},{7,5},{8,10},{9,11},{10,... | collective-permute-start | bytes 24584 | tf_op jit(solution)/shard_map/ppermute | solution.py:308
  23.9 2.4 %collective-permute-start.7 = (f32[16,128]{1,0:T(8,128)S(1)}, f32[16,128]{1,0:T(8,128)S(1)}, u32[]{:S(2)}, u32[]{:S(2)}) collective-permute-start(f32[16,128]{1,0:T(8,128)S(1)} %bitcast.96), channel_id=1, source_target_pairs={{0,1},{1,0},{2,3},{3,2},{4,5},{5,4},{6,7},{7,6},{8,9},{9,8},{10,11... | collective-permute-start | bytes 24584 | tf_op jit(solution)/shard_map/ppermute | solution.py:308
  30.3 1.3 %collective-permute-start.8 = (f32[144,128]{1,0:T(8,128)S(1)}, f32[144,128]{1,0:T(8,128)S(1)}, u32[]{:S(2)}, u32[]{:S(2)}) collective-permute-start(f32[144,128]{1,0:T(8,128)S(1)} %pad_maximum_fusion.3), channel_id=1, source_target_pairs={{0,1},{1,0},{2,3},{3,2},{4,5},{5,4},{6,7},{7,6},{8,9},{9,8},{10,11... | collective-permute-start | bytes 221192 | tf_op jit(solution)/shard_map/ppermute | solution.py:308
  31.7 6.9 %collective-permute-start.9 = (f32[144,128]{1,0:T(8,128)S(1)}, f32[144,128]{1,0:T(8,128)S(1)}, u32[]{:S(2)}, u32[]{:S(2)}) collective-permute-start(f32[144,128]{1,0:T(8,128)S(1)} %pad_maximum_fusion.4), channel_id=1, source_target_pairs={{0,2},{1,3},{2,0},{3,1},{4,6},{5,7},{6,4},{7,5},{8,10},{9,11},{10,... | collective-permute-start | bytes 221192 | tf_op jit(solution)/shard_map/ppermute | solution.py:308
  38.7 4.4 %collective-permute-start.10 = (f32[144,128]{1,0:T(8,128)S(1)}, f32[144,128]{1,0:T(8,128)S(1)}, u32[]{:S(2)}, u32[]{:S(2)}) collective-permute-start(f32[144,128]{1,0:T(8,128)S(1)} %pad_maximum_fusion.5), channel_id=1, source_target_pairs={{0,4},{1,5},{2,6},{3,7},{4,0},{5,1},{6,2},{7,3},{8,12},{9,13},{10,... | collective-permute-start | bytes 221192 | tf_op jit(solution)/shard_map/ppermute | solution.py:308
  43.2 5.6 %collective-permute-start.11 = (f32[144,128]{1,0:T(8,128)S(1)}, f32[144,128]{1,0:T(8,128)S(1)}, u32[]{:S(2)}, u32[]{:S(2)}) collective-permute-start(f32[144,128]{1,0:T(8,128)S(1)} %pad_maximum_fusion.6), channel_id=1, source_target_pairs={{0,12},{1,13},{2,14},{3,15},{4,8},{5,9},{6,10},{7,11},{8,4},{9,5},... | collective-permute-start | bytes 221192 | tf_op jit(solution)/shard_map/ppermute | solution.py:308
  48.8 4.3 %collective-permute-start.12 = (f32[128,128]{1,0:T(8,128)S(1)}, f32[128,128]{1,0:T(8,128)S(1)}, u32[]{:S(2)}, u32[]{:S(2)}) collective-permute-start(f32[128,128]{1,0:T(8,128)S(1)} %slice_add_fusion), channel_id=1, source_target_pairs={{0,64},{16,80},{32,96},{48,112},{64,0},{80,16},{96,32},{112,48},{1... | collective-permute-start | bytes 196616 | tf_op jit(solution)/shard_map/ppermute | solution.py:308
  53.2 4.3 %collective-permute-start.13 = (f32[128,128]{1,0:T(8,128)S(1)}, f32[128,128]{1,0:T(8,128)S(1)}, u32[]{:S(2)}, u32[]{:S(2)}) collective-permute-start(f32[128,128]{1,0:T(8,128)S(1)} %add.33), channel_id=1, source_target_pairs={{0,16},{16,0},{32,48},{48,32},{64,80},{80,64},{96,112},{112,96},{1... | collective-permute-start | bytes 196616 | tf_op jit(solution)/shard_map/ppermute | solution.py:308
  57.5 5.6 %collective-permute-start.14 = (f32[128,128]{1,0:T(8,128)S(1)}, f32[128,128]{1,0:T(8,128)S(1)}, u32[]{:S(2)}, u32[]{:S(2)}) collective-permute-start(f32[128,128]{1,0:T(8,128)S(1)} %add.34.mine), channel_id=1, source_target_pairs={{0,48},{16,32},{32,16},{48,0},{64,112},{80,96},{96,80},{112,64},{1... | collective-permute-start | bytes 196616 | tf_op jit(solution)/shard_map/ppermute | solution.py:308

commit v4 on v3

--- a/solution.py
+++ b/solution.py
@@ -68,25 +68,16 @@
     return value
 
 
-def prepare(
-    place, k1_hbm, b1_hbm, k2_hbm, b2_hbm, cot_hbm, left_one, left_two, left_back, send,
-    k1, b1, k2, b2, cot, sems,
-):
-    moves = [
-        pltpu.make_async_copy(source, target, sems.at[i])
-        for i, (source, target) in enumerate(
-            ((k1_hbm, k1), (b1_hbm, b1), (k2_hbm, k2), (b2_hbm, b2), (cot_hbm, cot))
-        )
-    ]
+def fetch(pairs, sems):
+    moves = [pltpu.make_async_copy(*pair, sems.at[i]) for i, pair in enumerate(pairs)]
     for move in moves:
         move.start()
     for move in moves:
         move.wait()
 
-    def ones_first(bias, rows):
-        row = iota((rows, bias.shape[1]), 0)
-        return jnp.where(row == 0, jnp.broadcast_to(bias, (rows, bias.shape[1])), 0.0)
-
+
+def arrange(place, cot_hbm, send, cot, sems):
+    fetch([(cot_hbm, cot)], sems)
     lower = iota((1, 128), 1) < 64
     rows = [None] * 32
     for f in range(2):
@@ -95,6 +86,17 @@
             rows[4 * k + f] = jnp.where(lower, near, pltpu.roll(far, 64, 1))
             rows[4 * k + 2 + f] = jnp.where(lower, pltpu.roll(near, 64, 1), far)
     send[...] = swap_last(xor_rows(jnp.concatenate(rows, axis=0), place[0], 2))
+
+
+def prepare(
+    k1_hbm, b1_hbm, k2_hbm, b2_hbm, slots, left_one, left_two, left_back, passed, k1, b1, k2, b2, sems
+):
+    passed[...] = slots[...]
+    fetch([(k1_hbm, k1), (b1_hbm, b1), (k2_hbm, k2), (b2_hbm, b2)], sems)
+
+    def ones_first(bias, rows):
+        row = iota((rows, bias.shape[1]), 0)
+        return jnp.where(row == 0, jnp.broadcast_to(bias, (rows, bias.shape[1])), 0.0)
 
     order = [(a * 3 + b) * 3 + c for a, b in TAPS_ONE for c in range(3)]
     taps = [jnp.concatenate([k1[t], k1[t]], axis=0) for t in order]
@@ -342,19 +344,13 @@
 
     k1 = jnp.transpose(kernel_one, (2, 3, 4, 1, 0)).reshape(27, 4, 16)
     k2 = jnp.transpose(kernel_two, (2, 3, 4, 1, 0)).reshape(27, 16, 32)
-    left_one, left_two, left_back, up = call(
-        prepare,
-        [((32, 224), BF16), ((64, 880), BF16), ((432, 128), BF16), ((32, 128), F32)],
-        [sm] + [pltpu.HBM] * 5,
-        [
-            ((27, 4, 16), F32),
-            ((1, 16), F32),
-            ((27, 16, 32), F32),
-            ((1, 32), F32),
-            ((2, 2, 1024), F32),
-            pltpu.SemaphoreType.DMA((5,)),
-        ],
-    )(place, *(pltpu.with_memory_space_constraint(v, pltpu.HBM) for v in (k1, bias_one[None], k2, bias_two[None], cotangent)))
+    in_hbm = lambda *values: [pltpu.with_memory_space_constraint(v, pltpu.HBM) for v in values]
+    (up,) = call(
+        arrange,
+        [((32, 128), F32)],
+        [sm, pltpu.HBM],
+        [((2, 2, 1024), F32), pltpu.SemaphoreType.DMA((1,))],
+    )(place, *in_hbm(cotangent))
 
     own = jnp.transpose(volume, (1, 2, 0, 3))
     xlo, xhi, _ = neighbours(own, "gx", 0)
@@ -362,7 +358,19 @@
     ylo, yhi, inner = neighbours(full, "gy", 1)
     turn_one = regroup(up, 3)
     turn_two = regroup(after(turn_one, inner), 2)
-    turn_three = regroup(turn_two, 1)
+    left_one, left_two, left_back, passed = call(
+        prepare,
+        [((32, 224), BF16), ((64, 880), BF16), ((432, 128), BF16), ((32, 128), F32)],
+        [pltpu.HBM] * 4 + [vm],
+        [
+            ((27, 4, 16), F32),
+            ((1, 16), F32),
+            ((27, 16, 32), F32),
+            ((1, 32), F32),
+            pltpu.SemaphoreType.DMA((4,)),
+        ],
+    )(*in_hbm(k1, bias_one[None], k2, bias_two[None]), turn_two)
+    turn_three = regroup(passed, 1)
     up = regroup(turn_three, 0)
 
     inside = lambda at, size, n: jnp.where(

time: 64.1 us -> 63.6 us (level)
  waiting for transfers between devices: 24.7 us -> 23.5 us
  Pallas kernels: 10.4 us -> 11.2 us
    ppermute x11, waiting for transfers between devices: 23.4 us -> 22.2 us  [flip(): lax.ppermute(value, axis, [(i, i ^ by) for i in range(lax.axis_size(axis))])]
    pallas_call x0 -> x1, Pallas kernels: none -> 0.83 us  [on_device(): call(arrange, [((32, 128), F32)], [sm, pltpu.HBM], [((2, 2, 1024), F32),...]
  transfers between devices with their start and end apart: 15 -> 15, of which waited for: 10 -> 10; matrix products, arithmetic and copies ran while one was open for 0% -> 0% of each run, Pallas kernels for 9% -> 10%
where the time goes in v4:
time: 63.6 us; the launch traced here: 63.4 us
  starting transfers between devices  26.3 us (41%)
  waiting for transfers between devices  23.5 us (37%)
  Pallas kernels  11.2 us (18%)
  local copies, waits for them, and re-layouts  1.09 us (2%)
  between operations  0.92 us (1%)
    ppermute x11, waiting for transfers between devices, flip(): lax.ppermute(value, axis, [(i, i ^ by) for i in range(lax.axis_size(axis))])  22.2 us
    ppermute x11, starting transfers between devices, flip(): lax.ppermute(value, axis, [(i, i ^ by) for i in range(lax.axis_size(axis))])  20.4 us
    ppermute x4, starting transfers between devices, swap(): return lax.ppermute(value, axis, pairs + [(j, i) for i, j in pairs])  5.96 us
    pallas_call x1, Pallas kernels, on_device(): call(backward, [((128, 128), F32)], [sm, sm] + [vm] * 6, [((432, 2048), F...  3.96 us
    pallas_call x1, Pallas kernels, on_device(): call(forward_one, [((224, 18432), BF16), ((12, 16, 1536), F32), ((6, 6, 9...  3.02 us
    pallas_call x1, Pallas kernels, on_device(): call(prepare, [((32, 224), BF16), ((64, 880), BF16), ((432, 128), BF16),...  1.36 us
  transfers between devices with their start and end apart: 15, of which 10 were waited for; matrix products, arithmetic and copies ran while one was open for 0% of the time, Pallas kernels for 10%

profile of v4, /device:TPU:0, one launch (start us, length us, event | category | flops | bytes accessed | tf_op | source)
XLA Modules:
  0.0 63.4 jit_solution(14796176896564278332)
XLA Ops:
  0.6 1.0 %copy.34 = f32[4,8,8,128]{3,0,2,1:T(4,128)S(1)} copy(f32[4,8,8,128]{3,2,1,0:T(8,128)} %param.6) | data formatting | bytes 262144 | tf_op args[0]
  2.3 4.6 %collective-permute-start = (f32[3,8,4,128]{3,2,1,0:T(4,128)S(1)}, f32[3,8,4,128]{3,2,1,0:T(4,128)S(1)}, u32[]{:S(2)}, u32[]{:S(2)}) collective-permute-start(f32[3,8,4,128]{3,2,1,0:T(4,128)S(1)} %get-tuple-element.40), channel_id=1, source_target_pairs={{0,16},{32,48},{64,80},{96,112},{16,0},{48,32},{80,64},{112,96},{1... | collective-permute-start | bytes 147464 | tf_op jit(solution)/shard_map/ppermute | solution.py:289
  6.9 0.8 %shard_map.101 = f32[32,128]{1,0:T(8,128)S(1)} custom-call(s32[1]{0:T(128)} %bitcast.place, f32[2,2,1024]{2,1,0:T(2,128)} %cot_hbm.1), custom_call_target="tpu_custom_call" | custom-call | flops 1000000 | bytes 1000000 | tf_op jit(solution)/shard_map/pallas_call | solution.py:348
  7.7 2.8 %collective-permute-start.4 = (f32[16,128]{1,0:T(8,128)S(1)}, f32[16,128]{1,0:T(8,128)S(1)}, u32[]{:S(2)}, u32[]{:S(2)}) collective-permute-start(f32[16,128]{1,0:T(8,128)S(1)} %get-tuple-element.58), channel_id=1, source_target_pairs={{0,12},{1,13},{2,14},{3,15},{4,8},{5,9},{6,10},{7,11},{8,4},{9,5},... | collective-permute-start | bytes 24584 | tf_op jit(solution)/shard_map/ppermute | solution.py:310
  10.8 1.3 %collective-permute-done.2 = f32[14,3,4,128]{3,2,1,0:T(4,128)S(1)} collective-permute-done((f32[14,3,4,128]{3,2,1,0:T(4,128)S(1)}, f32[14,3,4,128]{3,2,1,0:T(4,128)S(1)}, u32[]{:S(2)}, u32[]{:S(2)}) %collective-permute-start.2) | collective-permute-done | bytes 86048 | tf_op jit(solution)/shard_map/ppermute | solution.py:289
  13.7 2.6 %collective-permute-done.5 = f32[16,128]{1,0:T(8,128)S(1)} collective-permute-done((f32[16,128]{1,0:T(8,128)S(1)}, f32[16,128]{1,0:T(8,128)S(1)}, u32[]{:S(2)}, u32[]{:S(2)}) %collective-permute-start.5) | collective-permute-done | bytes 8224 | tf_op jit(solution)/shard_map/ppermute | solution.py:310
  16.4 1.4 %shard_map.102 = (bf16[32,224]{1,0:T(8,128)(2,1)S(1)}, bf16[64,880]{1,0:T(8,128)(2,1)S(1)}, bf16[432,128]{1,0:T(8,128)(2,1)S(1)}, f32[32,128]{1,0:T(8,128)S(1)}) custom-call(f32[27,4,16]{2,1,0:T(4,128)} %bitcast.85, f32[1,16]{1,0:T(1,128)} %bitcast.98, f32[27,16,32]{2,1,0:T(8,128)} %bitcast.82, f32[1,32]{1,0:T(1,128)} %bitcast.99, f32[32,128]{1,0:T(8,128)S(1)} %bitcast.75), custom_call_target="tpu_custom_call" | custom-call | flops 1000000 | bytes 1000000 | tf_op jit(solution)/shard_map/pallas_call | solution.py:361
  17.7 4.0 %collective-permute-start.6 = (f32[16,128]{1,0:T(8,128)S(1)}, f32[16,128]{1,0:T(8,128)S(1)}, u32[]{:S(2)}, u32[]{:S(2)}) collective-permute-start(f32[16,128]{1,0:T(8,128)S(1)} %bitcast.93), channel_id=1, source_target_pairs={{0,2},{1,3},{2,0},{3,1},{4,6},{5,7},{6,4},{7,5},{8,10},{9,11},{10,... | collective-permute-start | bytes 24584 | tf_op jit(solution)/shard_map/ppermute | solution.py:310
  21.7 3.0 %shard_map.103 = (bf16[224,18432]{1,0:T(8,128)(2,1)S(1)}, f32[12,16,1536]{2,1,0:T(8,128)S(1)}, bf16[6,6,96,128]{3,2,1,0:T(8,128)(2,1)S(1)}) custom-call(f32[16]{0:T(128)S(1)} %pad_maximum_fusion.13.edge, f32[3,8,4,128]{3,2,1,0:T(4,128)S(1)} %bitcast.72, f32[8,8,4,128]{3,2,1,0:T(4,128)S(1)} %bitcast.68, f32[3,8,4,128]{3,2,1,0:T(4,128)S(1)} %bitcast.70, ...), custom_call_target="tpu_custom_call" | custom-call | flops 10000000 | bytes 10000000 | tf_op jit(solution)/shard_map/pallas_call | solution.py:384
  24.9 1.3 %shard_map.104 = (bf16[880,2048]{1,0:T(8,128)(2,1)S(1)}, f32[4,32,512]{2,1,0:T(8,128)S(1)}, f32[32,128]{1,0:T(8,128)S(1)}) custom-call(s32[1]{0:T(128)} %bitcast.place, bf16[6,6,96,128]{3,2,1,0:T(8,128)(2,1)S(1)} %get-tuple-element.23.s_two, bf16[64,880]{1,0:T(8,128)(2,1)S(1)} %get-tuple-element.24.left_two, f32[32,128]{1,0:T(8,128)S(1)} %bitcast.74), custom_call_target="tpu_custom_call" | custom-call | flops 10000000 | bytes 10000000 | tf_op jit(solution)/shard_map/pallas_call | solution.py:391
  26.2 4.0 %shard_map.105 = f32[128,128]{1,0:T(8,128)S(1)} custom-call(s32[1]{0:T(128)} %bitcast.place, f32[16]{0:T(128)S(1)} %pad_maximum_fusion.13.edge, bf16[224,18432]{1,0:T(8,128)(2,1)S(1)} %get-tuple-element.21.p_one, f32[12,16,1536]{2,1,0:T(8,128)S(1)} %get-tuple-element.22.d_one, bf16[880,2048]{1,0:T(8,128)(2,1)S(1)} %get-tuple-element.26.p_two, ...), custom_call_target="tpu_custom_call" | custom-call | flops 10000000 | bytes 10000000 | tf_op jit(solution)/shard_map/pallas_call | solution.py:397
  30.7 0.9 %collective-permute-done.8 = f32[144,128]{1,0:T(8,128)S(1)} collective-permute-done((f32[144,128]{1,0:T(8,128)S(1)}, f32[144,128]{1,0:T(8,128)S(1)}, u32[]{:S(2)}, u32[]{:S(2)}) %collective-permute-start.8) | collective-permute-done | bytes 73760 | tf_op jit(solution)/shard_map/ppermute | solution.py:310
  31.7 3.5 %collective-permute-start.9 = (f32[144,128]{1,0:T(8,128)S(1)}, f32[144,128]{1,0:T(8,128)S(1)}, u32[]{:S(2)}, u32[]{:S(2)}) collective-permute-start(f32[144,128]{1,0:T(8,128)S(1)} %pad_maximum_fusion.4), channel_id=1, source_target_pairs={{0,2},{1,3},{2,0},{3,1},{4,6},{5,7},{6,4},{7,5},{8,10},{9,11},{10,... | collective-permute-start | bytes 221192 | tf_op jit(solution)/shard_map/ppermute | solution.py:310
  35.3 2.8 %collective-permute-done.9 = f32[144,128]{1,0:T(8,128)S(1)} collective-permute-done((f32[144,128]{1,0:T(8,128)S(1)}, f32[144,128]{1,0:T(8,128)S(1)}, u32[]{:S(2)}, u32[]{:S(2)}) %collective-permute-start.9) | collective-permute-done | bytes 73760 | tf_op jit(solution)/shard_map/ppermute | solution.py:310
  38.2 1.8 %collective-permute-start.10 = (f32[144,128]{1,0:T(8,128)S(1)}, f32[144,128]{1,0:T(8,128)S(1)}, u32[]{:S(2)}, u32[]{:S(2)}) collective-permute-start(f32[144,128]{1,0:T(8,128)S(1)} %pad_maximum_fusion.5), channel_id=1, source_target_pairs={{0,4},{1,5},{2,6},{3,7},{4,0},{5,1},{6,2},{7,3},{8,12},{9,13},{10,... | collective-permute-start | bytes 221192 | tf_op jit(solution)/shard_map/ppermute | solution.py:310
  40.0 2.6 %collective-permute-done.10 = f32[144,128]{1,0:T(8,128)S(1)} collective-permute-done((f32[144,128]{1,0:T(8,128)S(1)}, f32[144,128]{1,0:T(8,128)S(1)}, u32[]{:S(2)}, u32[]{:S(2)}) %collective-permute-start.10) | collective-permute-done | bytes 73760 | tf_op jit(solution)/shard_map/ppermute | solution.py:310
  42.6 2.6 %collective-permute-start.11 = (f32[144,128]{1,0:T(8,128)S(1)}, f32[144,128]{1,0:T(8,128)S(1)}, u32[]{:S(2)}, u32[]{:S(2)}) collective-permute-start(f32[144,128]{1,0:T(8,128)S(1)} %pad_maximum_fusion.6), channel_id=1, source_target_pairs={{0,12},{1,13},{2,14},{3,15},{4,8},{5,9},{6,10},{7,11},{8,4},{9,5},... | collective-permute-start | bytes 221192 | tf_op jit(solution)/shard_map/ppermute | solution.py:310
  45.3 3.0 %collective-permute-done.11 = f32[144,128]{1,0:T(8,128)S(1)} collective-permute-done((f32[144,128]{1,0:T(8,128)S(1)}, f32[144,128]{1,0:T(8,128)S(1)}, u32[]{:S(2)}, u32[]{:S(2)}) %collective-permute-start.11) | collective-permute-done | bytes 73760 | tf_op jit(solution)/shard_map/ppermute | solution.py:310
  48.3 1.3 %collective-permute-start.12 = (f32[128,128]{1,0:T(8,128)S(1)}, f32[128,128]{1,0:T(8,128)S(1)}, u32[]{:S(2)}, u32[]{:S(2)}) collective-permute-start(f32[128,128]{1,0:T(8,128)S(1)} %slice_add_fusion), channel_id=1, source_target_pairs={{0,64},{16,80},{32,96},{48,112},{64,0},{80,16},{96,32},{112,48},{1... | collective-permute-start | bytes 196616 | tf_op jit(solution)/shard_map/ppermute | solution.py:310
  49.6 3.0 %collective-permute-done.12 = f32[128,128]{1,0:T(8,128)S(1)} collective-permute-done((f32[128,128]{1,0:T(8,128)S(1)}, f32[128,128]{1,0:T(8,128)S(1)}, u32[]{:S(2)}, u32[]{:S(2)}) %collective-permute-start.12) | collective-permute-done | bytes 65568 | tf_op jit(solution)/shard_map/ppermute | solution.py:310
  53.5 3.5 %collective-permute-done.13 = f32[128,128]{1,0:T(8,128)S(1)} collective-permute-done((f32[128,128]{1,0:T(8,128)S(1)}, f32[128,128]{1,0:T(8,128)S(1)}, u32[]{:S(2)}, u32[]{:S(2)}) %collective-permute-start.13) | collective-permute-done | bytes 65568 | tf_op jit(solution)/shard_map/ppermute | solution.py:310
  57.0 2.5 %collective-permute-start.14 = (f32[128,128]{1,0:T(8,128)S(1)}, f32[128,128]{1,0:T(8,128)S(1)}, u32[]{:S(2)}, u32[]{:S(2)}) collective-permute-start(f32[128,128]{1,0:T(8,128)S(1)} %add.34.mine), channel_id=1, source_target_pairs={{0,48},{16,32},{32,16},{48,0},{64,112},{80,96},{96,80},{112,64},{1... | collective-permute-start | bytes 196616 | tf_op jit(solution)/shard_map/ppermute | solution.py:310
  59.5 3.0 %collective-permute-done.14.other = f32[128,128]{1,0:T(8,128)S(1)} collective-permute-done((f32[128,128]{1,0:T(8,128)S(1)}, f32[128,128]{1,0:T(8,128)S(1)}, u32[]{:S(2)}, u32[]{:S(2)}) %collective-permute-start.14) | collective-permute-done | bytes 65568 | tf_op jit(solution)/shard_map/ppermute | solution.py:310
  62.6 0.8 %shard_map.106 = (f32[2,2,1024]{2,1,0:T(2,128)}, f32[27,4,16]{2,1,0:T(4,128)}, f32[1,16]{1,0:T(1,128)}, f32[27,16,32]{2,1,0:T(8,128)}, f32[1,32]{1,0:T(1,128)}) custom-call(s32[1]{0:T(128)} %bitcast.place, f32[128,128]{1,0:T(8,128)S(1)} %add.34.mine, f32[128,128]{1,0:T(8,128)S(1)} %collective-permute-done.14.other, f32[32,128]{1,0:T(8,128)S(1)} %bitcast.78), custom_call_target="tpu_custom_call" | custom-call | flops 1000000 | bytes 1000000 | tf_op jit(solution)/shard_map/pallas_call | solution.py:415
  (56 shorter events, 4.2 us)
Async XLA Ops:
  1.7 8.9 %collective-permute-start.1 = (f32[3,8,4,128]{3,2,1,0:T(4,128)S(1)}, f32[3,8,4,128]{3,2,1,0:T(4,128)S(1)}, u32[]{:S(2)}, u32[]{:S(2)}) collective-permute-start(f32[3,8,4,128]{3,2,1,0:T(4,128)S(1)} %get-tuple-element.39), channel_id=1, source_target_pairs={{16,32},{48,64},{80,96},{32,16},{64,48},{96,80},{17,33},{49,65},{8... | collective-permute-start | bytes 147464 | tf_op jit(solution)/shard_map/ppermute | solution.py:289
  2.3 8.3 %collective-permute-start = (f32[3,8,4,128]{3,2,1,0:T(4,128)S(1)}, f32[3,8,4,128]{3,2,1,0:T(4,128)S(1)}, u32[]{:S(2)}, u32[]{:S(2)}) collective-permute-start(f32[3,8,4,128]{3,2,1,0:T(4,128)S(1)} %get-tuple-element.40), channel_id=1, source_target_pairs={{0,16},{32,48},{64,80},{96,112},{16,0},{48,32},{80,64},{112,96},{1... | collective-permute-start | bytes 147464 | tf_op jit(solution)/shard_map/ppermute | solution.py:289
  7.7 4.9 %collective-permute-start.4 = (f32[16,128]{1,0:T(8,128)S(1)}, f32[16,128]{1,0:T(8,128)S(1)}, u32[]{:S(2)}, u32[]{:S(2)}) collective-permute-start(f32[16,128]{1,0:T(8,128)S(1)} %get-tuple-element.58), channel_id=1, source_target_pairs={{0,12},{1,13},{2,14},{3,15},{4,8},{5,9},{6,10},{7,11},{8,4},{9,5},... | collective-permute-start | bytes 24584 | tf_op jit(solution)/shard_map/ppermute | solution.py:310
  10.7 1.4 %collective-permute-start.2 = (f32[14,3,4,128]{3,2,1,0:T(4,128)S(1)}, f32[14,3,4,128]{3,2,1,0:T(4,128)S(1)}, u32[]{:S(2)}, u32[]{:S(2)}) collective-permute-start(f32[14,3,4,128]{3,2,1,0:T(4,128)S(1)} %get-tuple-element.36), channel_id=1, source_target_pairs={{0,1},{2,3},{4,5},{6,7},{8,9},{10,11},{12,13},{14,15},{1,0},{3,2},... | collective-permute-start | bytes 258056 | tf_op jit(solution)/shard_map/ppermute | solution.py:289
  12.7 3.7 %collective-permute-start.5 = (f32[16,128]{1,0:T(8,128)S(1)}, f32[16,128]{1,0:T(8,128)S(1)}, u32[]{:S(2)}, u32[]{:S(2)}) collective-permute-start(f32[16,128]{1,0:T(8,128)S(1)} %get-tuple-element.56), channel_id=1, source_target_pairs={{0,4},{1,5},{2,6},{3,7},{4,0},{5,1},{6,2},{7,3},{8,12},{9,13},{10,... | collective-permute-start | bytes 24584 | tf_op jit(solution)/shard_map/ppermute | solution.py:310
  13.1 8.6 %collective-permute-start.3 = (f32[14,3,4,128]{3,2,1,0:T(4,128)S(1)}, f32[14,3,4,128]{3,2,1,0:T(4,128)S(1)}, u32[]{:S(2)}, u32[]{:S(2)}) collective-permute-start(f32[14,3,4,128]{3,2,1,0:T(4,128)S(1)} %get-tuple-element.35), channel_id=1, source_target_pairs={{1,2},{3,4},{5,6},{7,8},{9,10},{11,12},{13,14},{2,1},{4,3},{6,5},{... | collective-permute-start | bytes 258056 | tf_op jit(solution)/shard_map/ppermute | solution.py:289
  17.7 7.0 %collective-permute-start.6 = (f32[16,128]{1,0:T(8,128)S(1)}, f32[16,128]{1,0:T(8,128)S(1)}, u32[]{:S(2)}, u32[]{:S(2)}) collective-permute-start(f32[16,128]{1,0:T(8,128)S(1)} %bitcast.93), channel_id=1, source_target_pairs={{0,2},{1,3},{2,0},{3,1},{4,6},{5,7},{6,4},{7,5},{8,10},{9,11},{10,... | collective-permute-start | bytes 24584 | tf_op jit(solution)/shard_map/ppermute | solution.py:310
  24.8 1.4 %collective-permute-start.7 = (f32[16,128]{1,0:T(8,128)S(1)}, f32[16,128]{1,0:T(8,128)S(1)}, u32[]{:S(2)}, u32[]{:S(2)}) collective-permute-start(f32[16,128]{1,0:T(8,128)S(1)} %bitcast.97), channel_id=1, source_target_pairs={{0,1},{1,0},{2,3},{3,2},{4,5},{5,4},{6,7},{7,6},{8,9},{9,8},{10,11... | collective-permute-start | bytes 24584 | tf_op jit(solution)/shard_map/ppermute | solution.py:310
  30.2 1.5 %collective-permute-start.8 = (f32[144,128]{1,0:T(8,128)S(1)}, f32[144,128]{1,0:T(8,128)S(1)}, u32[]{:S(2)}, u32[]{:S(2)}) collective-permute-start(f32[144,128]{1,0:T(8,128)S(1)} %pad_maximum_fusion.3), channel_id=1, source_target_pairs={{0,1},{1,0},{2,3},{3,2},{4,5},{5,4},{6,7},{7,6},{8,9},{9,8},{10,11... | collective-permute-start | bytes 221192 | tf_op jit(solution)/shard_map/ppermute | solution.py:310
  31.7 6.3 %collective-permute-start.9 = (f32[144,128]{1,0:T(8,128)S(1)}, f32[144,128]{1,0:T(8,128)S(1)}, u32[]{:S(2)}, u32[]{:S(2)}) collective-permute-start(f32[144,128]{1,0:T(8,128)S(1)} %pad_maximum_fusion.4), channel_id=1, source_target_pairs={{0,2},{1,3},{2,0},{3,1},{4,6},{5,7},{6,4},{7,5},{8,10},{9,11},{10,... | collective-permute-start | bytes 221192 | tf_op jit(solution)/shard_map/ppermute | solution.py:310
  38.2 4.4 %collective-permute-start.10 = (f32[144,128]{1,0:T(8,128)S(1)}, f32[144,128]{1,0:T(8,128)S(1)}, u32[]{:S(2)}, u32[]{:S(2)}) collective-permute-start(f32[144,128]{1,0:T(8,128)S(1)} %pad_maximum_fusion.5), channel_id=1, source_target_pairs={{0,4},{1,5},{2,6},{3,7},{4,0},{5,1},{6,2},{7,3},{8,12},{9,13},{10,... | collective-permute-start | bytes 221192 | tf_op jit(solution)/shard_map/ppermute | solution.py:310
  42.6 5.6 %collective-permute-start.11 = (f32[144,128]{1,0:T(8,128)S(1)}, f32[144,128]{1,0:T(8,128)S(1)}, u32[]{:S(2)}, u32[]{:S(2)}) collective-permute-start(f32[144,128]{1,0:T(8,128)S(1)} %pad_maximum_fusion.6), channel_id=1, source_target_pairs={{0,12},{1,13},{2,14},{3,15},{4,8},{5,9},{6,10},{7,11},{8,4},{9,5},... | collective-permute-start | bytes 221192 | tf_op jit(solution)/shard_map/ppermute | solution.py:310
  48.3 4.3 %collective-permute-start.12 = (f32[128,128]{1,0:T(8,128)S(1)}, f32[128,128]{1,0:T(8,128)S(1)}, u32[]{:S(2)}, u32[]{:S(2)}) collective-permute-start(f32[128,128]{1,0:T(8,128)S(1)} %slice_add_fusion), channel_id=1, source_target_pairs={{0,64},{16,80},{32,96},{48,112},{64,0},{80,16},{96,32},{112,48},{1... | collective-permute-start | bytes 196616 | tf_op jit(solution)/shard_map/ppermute | solution.py:310
  52.7 4.3 %collective-permute-start.13 = (f32[128,128]{1,0:T(8,128)S(1)}, f32[128,128]{1,0:T(8,128)S(1)}, u32[]{:S(2)}, u32[]{:S(2)}) collective-permute-start(f32[128,128]{1,0:T(8,128)S(1)} %add.33), channel_id=1, source_target_pairs={{0,16},{16,0},{32,48},{48,32},{64,80},{80,64},{96,112},{112,96},{1... | collective-permute-start | bytes 196616 | tf_op jit(solution)/shard_map/ppermute | solution.py:310
  57.0 5.6 %collective-permute-start.14 = (f32[128,128]{1,0:T(8,128)S(1)}, f32[128,128]{1,0:T(8,128)S(1)}, u32[]{:S(2)}, u32[]{:S(2)}) collective-permute-start(f32[128,128]{1,0:T(8,128)S(1)} %add.34.mine), channel_id=1, source_target_pairs={{0,48},{16,32},{32,16},{48,0},{64,112},{80,96},{96,80},{112,64},{1... | collective-permute-start | bytes 196616 | tf_op jit(solution)/shard_map/ppermute | solution.py:310
